TPU v7x, 128 devices: a whole 4x4x4 slice. The times are simulated.
128 devices in a mesh: seq: 8 (over z, core), tp: 16 (over y, x).
Axes of the slice: x: 4, y: 4, z: 4, core: 2. Of those that a mesh axis runs over, the one named last changes fastest.
Arguments:
- block_input: float32 [2, 8192, 1024], P(None, 'seq'), may hold values from -6 to 6
- first_gain: float32 [1024], replicated, may hold values from 0.1 to 1.9
- in_weight: bfloat16 [1024, 3, 1024], P(None, None, 'tp'), may hold values from -0.1875 to 0.1875
- conv_taps: float32 [3, 1024], P(None, 'tp'), may hold values from -2.5 to 2.5
- out_weight: bfloat16 [1024, 1024], P('tp'), may hold values from -0.1875 to 0.1875
- second_gain: float32 [1024], replicated, may hold values from 0.1 to 1.9
- gate_weight: bfloat16 [1024, 4608], P(None, 'tp'), may hold values from -0.1875 to 0.1875
- up_weight: bfloat16 [1024, 4608], P(None, 'tp'), may hold values from -0.1875 to 0.1875
- down_weight: bfloat16 [4608, 1024], P('tp'), may hold values from -0.09375 to 0.09375
- doc_starts: int32 [2, 8], replicated, may hold values from 0 to 8191, as said below
- out_cotangent: float32 [2, 8192, 1024], P(None, 'seq'), may hold values from -6 to 6
Outputs:
- block_output: float32 [2, 8192, 1024], P(None, 'seq')
- input_grad: float32 [2, 8192, 1024], P(None, 'seq')
- first_gain_grad: float32 [1024], replicated
- in_weight_grad: float32 [1024, 3, 1024], P(None, None, 'tp')
- conv_taps_grad: float32 [3, 1024], P(None, 'tp')
- out_weight_grad: float32 [1024, 1024], P('tp')
- second_gain_grad: float32 [1024], replicated
- gate_weight_grad: float32 [1024, 4608], P(None, 'tp')
- up_weight_grad: float32 [1024, 4608], P(None, 'tp')
- down_weight_grad: float32 [4608, 1024], P('tp')
Inputs may be any that keep to these rules, and one draw needn't show every extreme that they name: `doc_starts`: each row lists the first positions of the 8 documents packed into one sequence, strictly increasing, the first one 0; the last document ends at 8192.
All inputs are finite; a program needn't handle non-finite values.
Results may differ from a plain program's by a relative error of at most 0.024.
Values may be sent and summed in bfloat16 or wider, within the bound.
No kernel may reach another device: no remote copies, remote signals or barrier semaphores. Data moves between devices by JAX's collectives and lax.ppermute only.
A program may use at most 192 MiB of HBM per device.

v0:
```python
import jax
import jax.numpy as jnp
from jax import lax
from jax.experimental import pallas as pl
from jax.experimental.pallas import tpu as pltpu
from jax.sharding import Mesh
from jax.sharding import PartitionSpec as P

epsilon = 1e-05
SEQ = ("z", "core")
TP = ("y", "x")
ALL = SEQ + TP
RING = 4
TPS = RING * RING
f32 = jnp.float32
bf16 = jnp.bfloat16


def turn(value, axis, steps):
    return lax.ppermute(value, axis, [(i, (i + steps) % RING) for i in range(RING)])


def ring_near(value, axis):
    return turn(value, axis, 3), turn(value, axis, 1)


def ring_far(near, axes):
    half = near[0].shape[0] // 2
    halves = assemble(
        near, (((1, 0, half),), ((0, half, half),), ((3, 0, half),), ((2, half, half),))
    )
    return tuple(turn(halves[i], axes[i // 2], (1, 3)[i % 2]) for i in range(4))


tied = lax.optimization_barrier


def plane_gather(value, early=(), launch=None, beside=()):
    half = value.shape[0] // 2
    top, bottom = assemble((value,), (((0, 0, half),), ((0, half, half),)))
    near = tuple(turn(top, "x", k) for k in (3, 2, 1)) + tuple(turn(bottom, "y", k) for k in (3, 2, 1))
    near, early = tied((near, early))
    launched, beside_last = launch(early) if launch else ((), ())
    top, bottom = assemble(
        (top, bottom) + near,
        (
            ((0, 0, half), (2, 0, half), (3, 0, half), (4, 0, half)),
            ((1, 0, half), (5, 0, half), (6, 0, half), (7, 0, half)),
        ),
    )
    near = ring_near(top, "y") + ring_near(bottom, "x")
    near, launched, beside = tied((near, launched, beside))
    far = ring_far(near, ("y", "x"))
    far, beside_last = tied((far, beside_last))
    return [top, near[0], near[1], bottom, near[2], near[3]], list(far), launched, beside_last, beside


def assemble(sources, plans):
    width, kind = sources[0].shape[1], sources[0].dtype
    copies = sum(len(plan) for plan in plans)

    def body(*refs):
        refs, sems = refs[:-1], refs[-1]
        started = []
        for out, plan in zip(refs[len(sources) :], plans):
            at = 0
            for source, start, rows in plan:
                copy = pltpu.make_async_copy(
                    refs[source].at[pl.ds(start, rows)],
                    out.at[pl.ds(at, rows)],
                    sems.at[len(started)],
                )
                copy.start()
                started.append(copy)
                at += rows
        for copy in started:
            copy.wait()

    shapes = [
        jax.ShapeDtypeStruct((sum(rows for _, _, rows in plan), width), kind) for plan in plans
    ]
    return pl.pallas_call(
        body,
        in_specs=[pl.BlockSpec(memory_space=pl.ANY)] * len(sources),
        out_specs=[pl.BlockSpec(memory_space=pl.ANY)] * len(plans),
        out_shape=shapes,
        scratch_shapes=[pltpu.SemaphoreType.DMA((copies,))],
        compiler_params=pltpu.CompilerParams(vmem_limit_bytes=2 * 1024 * 1024),
        cost_estimate=pl.CostEstimate(
            flops=0, bytes_accessed=4 * sum(x.size for x in shapes), transcendentals=0
        ),
        name="assemble",
    )(*sources)


def add_halves(blocks, moved):
    half, width = moved[0].shape
    count = len(blocks)

    def body(*refs):
        ins, more, outs = refs[:count], refs[count : 2 * count], refs[2 * count : 3 * count]
        held, added, in_sems, more_sems, out_sems = refs[3 * count :]

        def rows(ref, i):
            return ref.at[pl.ds(half * (i % 2), half)]

        loads = []
        for i in range(count):
            one = pltpu.make_async_copy(rows(ins[i], i), held.at[i], in_sems.at[i])
            two = pltpu.make_async_copy(more[i], added.at[i], more_sems.at[i])
            one.start()
            two.start()
            loads.append((one, two))
        stores = []
        for i in range(count):
            for load in loads[i]:
                load.wait()
            held[i] = (held[i].astype(f32) + added[i].astype(f32)).astype(bf16)
            store = pltpu.make_async_copy(held.at[i], rows(outs[i], i), out_sems.at[i])
            store.start()
            stores.append(store)
        for store in stores:
            store.wait()

    return pl.pallas_call(
        body,
        in_specs=[pl.BlockSpec(memory_space=pl.ANY)] * (2 * count),
        out_specs=[pl.BlockSpec(memory_space=pl.ANY)] * count,
        out_shape=[jax.ShapeDtypeStruct(x.shape, x.dtype) for x in blocks],
        input_output_aliases={i: i for i in range(count)},
        scratch_shapes=[
            pltpu.VMEM((count, half, width), bf16),
            pltpu.VMEM((count, half, width), bf16),
            pltpu.SemaphoreType.DMA((count,)),
            pltpu.SemaphoreType.DMA((count,)),
            pltpu.SemaphoreType.DMA((count,)),
        ],
        compiler_params=pltpu.CompilerParams(vmem_limit_bytes=8 * 1024 * 1024),
        cost_estimate=pl.CostEstimate(
            flops=count * half * width, bytes_accessed=6 * count * half * width, transcendentals=0
        ),
        name="add_halves",
    )(*blocks, *moved)


def scatter_far(pieces, axes):
    return tied(
        tuple(turn(pieces[i], axes[i // 2], (1, 3)[i % 2]) for i in range(4))
    )


def scatter_near(blocks, moved, axes):
    blocks = add_halves(blocks, moved)
    return tuple(turn(blocks[i], axes[i // 2], (1, 3)[i % 2]) for i in range(4))


def in_vmem(count):
    return [pl.BlockSpec(memory_space=pltpu.VMEM)] * count


def whole(*shapes):
    return [
        pl.BlockSpec(
            shape, lambda *_, rank=len(shape): (0,) * rank, pipeline_mode=pl.Buffered(buffer_count=1)
        )
        for shape in shapes
    ]


def hbm_call(body, operands, outs, megabytes, flops, name):
    def outer(*refs):
        n, m = len(operands), len(outs)
        held, held_outs = refs[n + m : 2 * n + m], refs[2 * n + m : 2 * n + 2 * m]
        sems = refs[-1]
        loads = [pltpu.make_async_copy(refs[i], held[i], sems.at[i]) for i in range(n)]
        for load in loads:
            load.start()
        for load in loads:
            load.wait()
        body(*held, *held_outs)
        stores = [
            pltpu.make_async_copy(held_outs[i], refs[n + i], sems.at[n + i]) for i in range(m)
        ]
        for store in stores:
            store.start()
        for store in stores:
            store.wait()

    arrays = list(operands) + list(outs)
    return pl.pallas_call(
        outer,
        in_specs=[pl.BlockSpec(memory_space=pltpu.HBM)] * len(operands),
        out_specs=[pl.BlockSpec(memory_space=pltpu.HBM)] * len(outs),
        out_shape=list(outs),
        scratch_shapes=[pltpu.VMEM(x.shape, x.dtype) for x in arrays]
        + [pltpu.SemaphoreType.DMA((len(arrays),))],
        compiler_params=pltpu.CompilerParams(vmem_limit_bytes=megabytes * 1024 * 1024),
        cost_estimate=pl.CostEstimate(
            flops=flops,
            bytes_accessed=sum(x.size * x.dtype.itemsize for x in arrays),
            transcendentals=0,
        ),
        name=name,
    )(*operands)


def ring_sums(own, one, other):
    rows, width = own.shape
    step = rows // RING
    cuts = tuple(step * k for k in range(RING + 1))

    def body(own_ref, one_ref, other_ref, *outs):
        for out, low, high in zip(outs, cuts[:-1], cuts[1:]):
            total = own_ref[low:high, :].astype(f32) + (
                one_ref[low:high, :].astype(f32) + other_ref[low:high, :].astype(f32)
            )
            out[...] = total.astype(out.dtype)

    return pl.pallas_call(
        body,
        grid=(1,),
        in_specs=whole(*[own.shape] * 3),
        out_specs=whole(*((high - low, width) for low, high in zip(cuts[:-1], cuts[1:]))),
        out_shape=[
            jax.ShapeDtypeStruct((high - low, width), f32 if low == 0 else bf16)
            for low, high in zip(cuts[:-1], cuts[1:])
        ],
        compiler_params=pltpu.CompilerParams(vmem_limit_bytes=10 * 1024 * 1024),
        cost_estimate=pl.CostEstimate(
            flops=2 * rows * width, bytes_accessed=8 * rows * width, transcendentals=0
        ),
        name="ring_sums",
    )(own, one, other)


def swap_cores(value):
    return lax.ppermute(value, "core", [(0, 1), (1, 0)])


CHUNKS = ((0, 0), (0, 1), (0, 3), (1, 0), (1, 1), (1, 3), (0, 2), (1, 2))


def plane_starts(half):
    y, x = lax.axis_index("y"), lax.axis_index("x")
    side = jnp.array([s for s, _ in CHUNKS for _ in range(RING)], jnp.int32)
    outer = jnp.array([k for _, k in CHUNKS for _ in range(RING)], jnp.int32)
    inner = jnp.array([k for _ in CHUNKS for k in range(RING)], jnp.int32)
    row = (jnp.where(side == 0, outer, inner) + y) % RING
    column = (jnp.where(side == 0, inner, outer) + x) % RING
    return (2 * (row * RING + column) + side) * half


def relative_rows(rows, starts, weight, split):
    half, width = rows.shape[0] // TPS // 2, rows.shape[1]
    count, units = rows.shape[0], weight.shape[0]
    slots = 8

    def body(table, source, weight_ref, low_a, low_b, hidden_a, hidden_b, held, lows, hiddens, *sems):
        sems, low_sems, hidden_sems = sems
        def copy(i):
            start = pl.multiple_of(table[i], half)
            return pltpu.make_async_copy(
                source.at[pl.ds(start, half)], held.at[i % slots], sems.at[i % slots]
            )

        for i in range(slots):
            copy(i).start()
        outs = []
        for i in range(0, 2 * TPS, RING):
            parts = []
            for j in range(i, i + RING):
                copy(j).wait()
                parts.append(held[j % slots].astype(bf16))
            low = jnp.concatenate(parts, axis=0)
            for j in range(i + slots, min(i + slots + RING, 2 * TPS)):
                copy(j).start()
            at, k = i * half, i // RING
            to_low, to_hidden = (low_a, hidden_a) if at < split else (low_b, hidden_b)
            at = at if at < split else at - split
            lows[k] = low
            hiddens[k] = dot(low, weight_ref[...], 1, 1)
            rows = pl.ds(at, RING * half)
            out = pltpu.make_async_copy(lows.at[k], to_low.at[rows], low_sems.at[k])
            out.start()
            outs.append(out)
            out = pltpu.make_async_copy(hiddens.at[k], to_hidden.at[rows], hidden_sems.at[k])
            out.start()
            outs.append(out)
        for out in outs:
            out.wait()

    return pl.pallas_call(
        body,
        grid_spec=pltpu.PrefetchScalarGridSpec(
            num_scalar_prefetch=1,
            grid=(1,),
            in_specs=[
                pl.BlockSpec(memory_space=pltpu.HBM),
                pl.BlockSpec(memory_space=pltpu.VMEM),
            ],
            out_specs=[pl.BlockSpec(memory_space=pltpu.HBM)] * 4,
            scratch_shapes=[
                pltpu.VMEM((slots, half, width), f32),
                pltpu.VMEM((2 * TPS // RING, RING * half, width), bf16),
                pltpu.VMEM((2 * TPS // RING, RING * half, units), f32),
                pltpu.SemaphoreType.DMA((slots,)),
                pltpu.SemaphoreType.DMA((2 * TPS // RING,)),
                pltpu.SemaphoreType.DMA((2 * TPS // RING,)),
            ],
        ),
        out_shape=[
            jax.ShapeDtypeStruct((split, width), bf16),
            jax.ShapeDtypeStruct((count - split, width), bf16),
            jax.ShapeDtypeStruct((split, units), f32),
            jax.ShapeDtypeStruct((count - split, units), f32),
        ],
        compiler_params=pltpu.CompilerParams(vmem_limit_bytes=16 * 1024 * 1024),
        cost_estimate=pl.CostEstimate(
            flops=2 * rows.size * units, bytes_accessed=rows.size * 6, transcendentals=0
        ),
        name="relative_rows",
    )(starts, rows, weight)


def absolute_rows(chunks, starts):
    total, width = sum(chunk.shape[0] for chunk in chunks), chunks[0].shape[1]
    half = total // TPS // 2
    slots = 16
    pieces = [(k, j) for k, chunk in enumerate(chunks) for j in range(chunk.shape[0] // half)]

    def body(table, *refs):
        parts, out, held, sems = refs[: len(chunks)], refs[-3], refs[-2], refs[-1]

        def copy(i):
            start = pl.multiple_of(table[i], half)
            return pltpu.make_async_copy(
                held.at[i % slots], out.at[pl.ds(start, half)], sems.at[i % slots]
            )

        for i, (k, j) in enumerate(pieces):
            if i >= slots:
                copy(i - slots).wait()
            held[i % slots] = parts[k][j * half : (j + 1) * half, :].astype(f32)
            copy(i).start()
        for i in range(2 * TPS - slots, 2 * TPS):
            copy(i).wait()

    return pl.pallas_call(
        body,
        grid_spec=pltpu.PrefetchScalarGridSpec(
            num_scalar_prefetch=1,
            grid=(1,),
            in_specs=[pl.BlockSpec(memory_space=pltpu.VMEM)] * len(chunks),
            out_specs=pl.BlockSpec(memory_space=pl.ANY),
            scratch_shapes=[
                pltpu.VMEM((slots, half, width), f32),
                pltpu.SemaphoreType.DMA((slots,)),
            ],
        ),
        out_shape=jax.ShapeDtypeStruct((total, width), f32),
        compiler_params=pltpu.CompilerParams(vmem_limit_bytes=7 * 1024 * 1024),
        cost_estimate=pl.CostEstimate(
            flops=total * width, bytes_accessed=total * width * 6, transcendentals=0
        ),
        name="absolute_rows",
    )(starts, *chunks)


def norm_and_project(rows, gain, weight):
    count, width = rows.shape
    chans = weight.shape[0]
    step = 256

    def body(rows_ref, gain_ref, weight_ref, normed_ref, out_ref):
        block = rows_ref[...]
        inverse = lax.rsqrt(jnp.mean(block * block, axis=-1, keepdims=True) + epsilon)
        normed = (block * inverse * gain_ref[...]).astype(bf16)
        normed_ref[...] = normed
        out_ref[...] = dot(weight_ref[...], normed, 1, 1)

    return pl.pallas_call(
        body,
        grid=(count // step,),
        in_specs=[
            pl.BlockSpec((step, width), lambda i: (i, 0)),
            pl.BlockSpec((1, width), lambda i: (0, 0)),
            pl.BlockSpec((chans, width), lambda i: (0, 0)),
        ],
        out_specs=[
            pl.BlockSpec((step, width), lambda i: (i, 0)),
            pl.BlockSpec((chans, step), lambda i: (0, i)),
        ],
        out_shape=[
            jax.ShapeDtypeStruct((count, width), bf16),
            jax.ShapeDtypeStruct((chans, count), f32),
        ],
        compiler_params=pltpu.CompilerParams(vmem_limit_bytes=6 * 1024 * 1024),
        cost_estimate=pl.CostEstimate(
            flops=2 * count * width * chans, bytes_accessed=6 * count * width, transcendentals=0
        ),
        name="norm_and_project",
    )(rows, gain.reshape(1, width), weight)


def mixer_gates(rows, weight, taps, mask_one, mask_two):
    own, width = mask_one.shape[0], rows.shape[1]
    chans = taps.shape[1]

    def body(rows_ref, weight_ref, taps_ref, one_ref, two_ref, gates_ref, lags_ref, conv_ref):
        b_gate = dot(rows_ref[...], weight_ref[:chans, :], 1, 1)
        c_gate = dot(rows_ref[8:, :], weight_ref[chans : 2 * chans, :], 1, 1)
        x_gate = dot(rows_ref[...], weight_ref[2 * chans :, :], 1, 1)
        product = (b_gate * x_gate).astype(bf16).astype(f32)
        one = one_ref[...] * product[7 : 7 + own]
        two = two_ref[...] * product[6 : 6 + own]
        product = product[8:]
        gates_ref[0] = b_gate[8:]
        gates_ref[1] = c_gate
        gates_ref[2] = x_gate[8:]
        lags_ref[0] = product
        lags_ref[1] = one
        lags_ref[2] = two
        conv_ref[...] = taps_ref[0:1, :] * product + taps_ref[1:2, :] * one + taps_ref[2:3, :] * two

    operands = (rows, weight, taps, mask_one, mask_two)
    outs = [
        jax.ShapeDtypeStruct((3, own, chans), f32),
        jax.ShapeDtypeStruct((3, own, chans), f32),
        jax.ShapeDtypeStruct((own, chans), f32),
    ]
    return pl.pallas_call(
        body,
        grid=(1,),
        in_specs=whole(*(x.shape for x in operands)),
        out_specs=whole(*(x.shape for x in outs)),
        out_shape=outs,
        compiler_params=pltpu.CompilerParams(vmem_limit_bytes=28 * 1024 * 1024),
        cost_estimate=pl.CostEstimate(
            flops=6 * own * width * chans, bytes_accessed=6 * width * chans, transcendentals=0
        ),
        name="mixer_gates",
    )(*operands)


def residual_back(own_sums, moved, residual, inverse, gain, grad, weight, c_rows, mask_one, mask_two):
    own, width = residual.shape
    half = own // 2
    chans = weight.shape[0]

    def body(*refs):
        sums, moved_refs, refs = refs[:2], refs[2:8], refs[8:]
        res_ref, inv_ref, gain_ref, grad_ref, weight_ref, gates_ref, one_ref, two_ref = refs[:8]
        block_ref, d_res_ref, low_ref, part_ref, mixer_ref, edge_ref = refs[8:]
        parts = []
        for i in range(2):
            rows = slice(i * half, (i + 1) * half)
            total = sums[i][...]
            for part in moved_refs[3 * i : 3 * i + 3]:
                total = total + part[...].astype(f32)
            d_norm, ffn = total[:, :width], total[:, width:]
            res, inv = res_ref[rows, :], inv_ref[rows, :]
            block_ref[rows, :] = (res + ffn).astype(bf16)
            parts.append(jnp.sum(d_norm * res * inv, axis=0, keepdims=True))
            scaled = gain_ref[...] * d_norm
            mean = jnp.mean(scaled * res, axis=-1, keepdims=True)
            d_res = grad_ref[rows, :] + inv * (scaled - res * inv * inv * mean)
            d_res_ref[rows, :] = d_res
            low_ref[rows, :] = d_res.astype(bf16)
        part_ref[...] = parts[0] + parts[1]
        d_mixer = dot(low_ref[...], weight_ref[...], 1, 1)
        mixer_ref[...] = d_mixer
        d_conv = d_mixer[:8] * gates_ref[...]
        edge_ref[0:8, :] = one_ref[:8, :] * d_conv
        edge_ref[8:16, :] = two_ref[:8, :] * d_conv

    operands = (*own_sums, *moved, residual, inverse, gain, grad, weight, c_rows, mask_one, mask_two)
    outs = [
        jax.ShapeDtypeStruct((own, width), bf16),
        jax.ShapeDtypeStruct((own, width), f32),
        jax.ShapeDtypeStruct((own, width), bf16),
        jax.ShapeDtypeStruct((1, width), f32),
        jax.ShapeDtypeStruct((own, chans), f32),
        jax.ShapeDtypeStruct((16, chans), f32),
    ]
    return hbm_call(body, operands, outs, 60, 2 * own * width * chans, "residual_back")


def mixer_back(
    d_mixer, edges, gates, lags, conv, mask_one, mask_two, taps, weight, rows, gain, d_res, second, halves
):
    own, width = rows.shape
    chans = d_mixer.shape[1]
    per = chans // TPS
    extra = 2 * width // own + 8

    def body(*refs):
        mixer_ref, edge_ref, gates_ref, lags_ref, conv_ref, one_ref, two_ref = refs[:7]
        taps_ref, weight_ref, rows_ref, gain_ref, d_res_ref, second_ref, halves_ref = refs[7:14]
        out_ref, send_ref, grads_ref = refs[14:]
        d_mix = mixer_ref[...]
        d_conv = d_mix * gates_ref[1]
        lag_one = one_ref[...] * d_conv
        lag_two = two_ref[...] * d_conv
        ahead_one = jnp.concatenate([lag_one[1:], edge_ref[0:1, :]], axis=0)
        ahead_two = jnp.concatenate([lag_two[2:], edge_ref[8:10, :]], axis=0)
        d_product = (
            taps_ref[0:1, :] * d_conv + taps_ref[1:2, :] * ahead_one + taps_ref[2:3, :] * ahead_two
        )
        grads_ref[0] = (d_product * gates_ref[2]).astype(bf16)
        grads_ref[1] = (d_mix * conv_ref[...]).astype(bf16)
        grads_ref[2] = (d_product * gates_ref[0]).astype(bf16)
        d_norm = dot(grads_ref[0], weight_ref[:chans, :], 1, 0)
        d_norm = d_norm + dot(grads_ref[1], weight_ref[chans : 2 * chans, :], 1, 0)
        d_norm = d_norm + dot(grads_ref[2], weight_ref[2 * chans :, :], 1, 0)
        block = rows_ref[...]
        inverse = lax.rsqrt(jnp.mean(block * block, axis=-1, keepdims=True) + epsilon)
        first = jnp.sum(d_norm * block * inverse, axis=0, keepdims=True)
        scaled = gain_ref[...] * d_norm
        mean = jnp.mean(scaled * block, axis=-1, keepdims=True)
        out = d_res_ref[...] + inverse * (scaled - block * inverse * inverse * mean)
        out_ref[...] = out.astype(bf16)
        tap_sums = [jnp.sum(d_conv * lags_ref[k], axis=0, keepdims=True) for k in range(3)]
        sums = jnp.concatenate(tap_sums + [jnp.zeros((5, chans), f32)], axis=0)
        gains = []
        for value in (first, second_ref[...]):
            gains += [value[:, k * own : (k + 1) * own] for k in range(width // own)]
        gains = jnp.concatenate(gains, axis=0)
        for g in range(3):
            turned = grads_ref[g].astype(f32).T.astype(bf16)
            for j in range(TPS):
                send_ref[j, g * per : (g + 1) * per, :] = turned[j * per : (j + 1) * per]
        for j in range(TPS):
            pair = j // 2 * 2 * per
            tail = jnp.concatenate([gains, sums[:, pair : pair + 2 * per]], axis=0)
            send_ref[j, 3 * per : 3 * per + extra, :] = tail.astype(bf16)
            for k in range(width // own):
                at = 3 * per + extra + k * halves.shape[1]
                send_ref[j, at : at + halves.shape[1], :] = halves_ref[j, :, k * own : (k + 1) * own]

    operands = (d_mixer, edges, gates, lags, conv, mask_one, mask_two, taps, weight, rows, gain, d_res, second, halves)
    outs = [
        jax.ShapeDtypeStruct((own, width), bf16),
        jax.ShapeDtypeStruct((TPS, 3 * per + extra + halves.shape[1] * width // own, own), bf16),
    ]
    return pl.pallas_call(
        body,
        grid=(1,),
        in_specs=whole(*(x.shape for x in operands)),
        out_specs=whole(*(x.shape for x in outs)),
        out_shape=outs,
        scratch_shapes=[pltpu.VMEM((3, own, chans), bf16)],
        compiler_params=pltpu.CompilerParams(vmem_limit_bytes=36 * 1024 * 1024),
        cost_estimate=pl.CostEstimate(
            flops=6 * own * width * chans, bytes_accessed=6 * width * chans, transcendentals=0
        ),
        name="mixer_back",
    )(*operands)


def feed_forward(norms, d_hidden, gate_t, up_t, down, pieces):
    count, ff = d_hidden.shape
    width = down.shape[1]
    step = norms[0].shape[0]
    piece = count // pieces

    def body(*refs):
        norm_refs, rest = refs[: len(norms)], refs[len(norms) :]
        d_hbm, gate_ref, up_ref, down_ref = rest[:4]
        outs, (d_gate_ref, d_up_ref, hidden_ref, d_ref, sem) = rest[4:-5], rest[-5:]
        load = pltpu.make_async_copy(d_hbm, d_ref, sem)
        load.start()
        for k, norm_ref in enumerate(norm_refs):
            part = slice(k * step, (k + 1) * step)
            norm = norm_ref[...]
            gate = dot(norm, gate_ref[...], 1, 1)
            up = dot(norm, up_ref[...], 1, 1)
            if k == 0:
                load.wait()
            d_part = d_ref[part, :]
            sig = jax.nn.sigmoid(gate)
            act = gate * sig
            hidden = (act * up).astype(bf16)
            d_gate = (d_part * up * sig * (1.0 + gate * (1.0 - sig))).astype(bf16)
            d_up = (d_part * act).astype(bf16)
            d_gate_ref[part, :] = d_gate
            d_up_ref[part, :] = d_up
            hidden_ref[part, :] = hidden
            d_norm = (dot(d_gate, gate_ref[...], 1, 0) + dot(d_up, up_ref[...], 1, 0)).astype(bf16)
            ffn = dot(hidden, down_ref[...], 1, 0, bf16)
            first = k * step // piece
            for j in range(max(1, step // piece)):
                inside = slice(j * piece, (j + 1) * piece)
                outs[first + j][:, :width] = d_norm[inside]
                outs[first + j][:, width:] = ffn[inside]

    outs = pl.pallas_call(
        body,
        in_specs=in_vmem(len(norms)) + [pl.BlockSpec(memory_space=pltpu.HBM)] + in_vmem(3),
        out_specs=in_vmem(pieces + 3),
        out_shape=[jax.ShapeDtypeStruct((piece, 2 * width), bf16)] * pieces
        + [jax.ShapeDtypeStruct((count, ff), bf16)] * 3,
        scratch_shapes=[pltpu.VMEM(d_hidden.shape, f32), pltpu.SemaphoreType.DMA(())],
        compiler_params=pltpu.CompilerParams(vmem_limit_bytes=12 * 1024 * 1024),
        cost_estimate=pl.CostEstimate(
            flops=10 * count * width * ff,
            bytes_accessed=count * width * 6,
            transcendentals=count * ff,
        ),
        name="feed_forward",
    )(*norms, d_hidden, gate_t, up_t, down)
    return outs[:pieces], outs[pieces:]


def dot(left, right, left_dim, right_dim, kind=f32):
    out = lax.dot_general(
        left, right, (((left_dim,), (right_dim,)), ((), ())), preferred_element_type=f32
    )
    return out.astype(kind)


def doc_index(doc_starts, positions):
    hits = (doc_starts[:, None, :] <= positions[None, :, None]).astype(jnp.int32)
    return jnp.sum(hits, axis=-1) - 1


def shards(
    block_input,
    first_gain,
    in_weight,
    conv_taps,
    out_weight,
    second_gain,
    gate_weight,
    up_weight,
    down_weight,
    doc_starts,
    out_cotangent,
):
    seqs, seg, width = block_input.shape
    chans = in_weight.shape[2]
    ff = gate_weight.shape[1]
    count = seqs * seg
    own = count // TPS
    per_seq = TPS // seqs
    y, x = lax.axis_index("y"), lax.axis_index("x")
    place = y * RING + x
    seq = lax.axis_index(SEQ)
    starts = plane_starts(own // 2)

    positions = seq * seg + jnp.arange(seg, dtype=jnp.int32)
    current = doc_index(doc_starts, positions)
    one_back = (doc_index(doc_starts, positions - 1) == current).astype(f32)
    two_back = (doc_index(doc_starts, positions - 2) == current).astype(f32)

    channels = TPS * chans
    is_low = lax.axis_index("core") == 0
    out_half = lax.dynamic_slice_in_dim(
        out_weight, lax.axis_index("core") * (chans // 2), chans // 2, axis=0
    )
    out_mine = jnp.broadcast_to(out_half[None], (TPS, chans // 2, width))
    out_mine = lax.all_to_all(out_mine, TP, 0, 0, tiled=True)
    in_wt = jnp.transpose(in_weight, (1, 2, 0))
    share = chans // 8
    taps_high = lax.reduce_precision(conv_taps, 8, 7)
    taps_mid = lax.reduce_precision(conv_taps - taps_high, 8, 7)
    taps_low = lax.reduce_precision(conv_taps - taps_high - taps_mid, 8, 7)
    taps_row = jnp.stack([taps_high, taps_mid, taps_low], axis=0).astype(bf16).reshape(1, 9 * chans)
    taps_row = jnp.pad(taps_row, ((0, share - 1), (0, width - 9 * chans)))
    in_share = lax.dynamic_slice_in_dim(in_wt, seq * share, share, axis=1)
    in_share = jnp.concatenate([in_share, taps_row[None]], axis=0)
    in_all = lax.all_gather(in_share, ALL, axis=0, tiled=False)
    in_all = in_all.reshape(8, TPS, 4, share, width)
    taps = in_all[0, :, 3, 0, : 9 * chans].astype(f32).reshape(TPS, 3, 3, chans)
    taps = (taps[:, 0] + taps[:, 1]) + taps[:, 2]
    taps = taps.transpose(1, 0, 2).reshape(3, channels)
    in_all = in_all[:, :, :3].transpose(2, 1, 0, 3, 4).reshape(3 * channels, width)

    flat_input = block_input.reshape(count, width)
    in_flat = in_wt.reshape(3 * chans, width)
    normed1, projected = norm_and_project(flat_input, first_gain, in_flat)
    projected, out_mine = tied((projected, out_mine))
    out_theirs = swap_cores(out_mine)
    out_all = jnp.stack(
        [jnp.where(is_low, out_mine, out_theirs), jnp.where(is_low, out_theirs, out_mine)], axis=1
    ).reshape(channels, width)
    last = normed1.reshape(seqs, seg, width)[:, seg - 8 :]
    carried = lax.ppermute(
        last, ALL, [(i, i + TPS) for i in range(7 * TPS)]
    )
    mixer_blocks = []
    for s in range(seqs):
        proj = projected[:, s * seg : (s + 1) * seg]
        edge = dot(in_flat, carried[s], 1, 1)
        product = (proj[:chans] * proj[2 * chans :]).astype(bf16)
        before = (edge[:chans] * edge[2 * chans :]).astype(bf16)
        extended = jnp.concatenate([before[:, 6:], product], axis=1).astype(f32)
        convolved = (
            conv_taps[0][:, None] * product.astype(f32)
            + conv_taps[1][:, None] * one_back[s] * extended[:, 1 : seg + 1]
            + conv_taps[2][:, None] * two_back[s] * extended[:, :seg]
        )
        mixed = (proj[chans : 2 * chans] * convolved).astype(bf16)
        mixer_blocks.append(mixed.reshape(chans, per_seq, own).transpose(1, 0, 2))
    mixer_blocks = jnp.concatenate(mixer_blocks, axis=0)
    mixer = lax.all_to_all(mixer_blocks, TP, 0, 0, tiled=True)
    mixer = mixer.reshape(channels, own)

    rows_in = lax.dynamic_slice_in_dim(flat_input, place * own, own, axis=0)
    residual = rows_in + dot(mixer, out_all, 0, 0)
    inverse_two = lax.rsqrt(jnp.mean(residual * residual, axis=-1, keepdims=True) + epsilon)
    normed2 = (residual * inverse_two * second_gain).astype(bf16)

    later = (normed2[0, 0].astype(f32) * 0.0).astype(jnp.int32)
    split = count * 3 // 4
    *grad_low, hidden_first, hidden_last = relative_rows(
        out_cotangent.reshape(count, width), starts + later, down_weight, split
    )
    gate_t, up_t = gate_weight.T, up_weight.T
    norm_first, norm_last, _, _, (hidden_first, hidden_last) = plane_gather(
        normed2, beside=(hidden_first, hidden_last)
    )
    sums_first, kept_first = feed_forward(
        norm_first, hidden_first, gate_t, up_t, down_weight, 6
    )
    piece = norm_last[0].shape[0]
    norm_last = assemble(
        norm_last, (((0, 0, piece), (1, 0, piece)), ((2, 0, piece), (3, 0, piece)))
    )
    norm_last, sums_first = tied((norm_last, sums_first))
    sums_last, kept_last = feed_forward(norm_last, hidden_last, gate_t, up_t, down_weight, 4)
    moved = scatter_far(sums_last, ("y", "x"))
    moved, kept_first, kept_last, norm_first, norm_last = tied(
        (moved, kept_first, kept_last, norm_first, norm_last)
    )
    rows = norm_last[0].shape[0]
    norm_first, norm_last = assemble(
        tuple(norm_first) + tuple(norm_last),
        (tuple((i, 0, rows) for i in range(6)), ((6, 0, rows), (7, 0, rows))),
    )
    ffn_grads = []
    for k in range(3):
        right_first = norm_first if k < 2 else grad_low[0]
        right_last = norm_last if k < 2 else grad_low[1]
        part = dot(kept_first[k], right_first, 0, 0) + dot(kept_last[k], right_last, 0, 0)
        ffn_grads.append(part.astype(bf16))
    ffn_grads = jnp.concatenate(ffn_grads + [jnp.zeros((32, width), bf16)], axis=0)
    ffn_grads = lax.psum_scatter(ffn_grads, SEQ, scatter_dimension=0, tiled=True)

    rows_n1 = lax.dynamic_slice_in_dim(normed1, place * own, own, axis=0)
    local_edge = lax.dynamic_slice_in_dim(normed1, place * own - 8, 8, axis=0)
    at_start = place % per_seq == 0
    edge_n1 = jnp.where(at_start, carried[place // per_seq], local_edge)
    rows_one = lax.dynamic_slice_in_dim(one_back.reshape(count, 1), place * own, own, axis=0)
    rows_two = lax.dynamic_slice_in_dim(two_back.reshape(count, 1), place * own, own, axis=0)
    rows_n1 = jnp.concatenate([edge_n1, rows_n1], axis=0)

    moved = scatter_near([sums_first[i] for i in (1, 2, 4, 5)], moved, ("y", "x"))
    gates, lags, conv = mixer_gates(rows_n1, in_all, taps, rows_one, rows_two)
    moved, gates, lags, conv = tied((moved, gates, lags, conv))
    top = ring_sums(sums_first[0], *moved[:2])
    bottom = ring_sums(sums_first[3], *moved[2:])
    moved = tuple(turn(top[k], "x", k) for k in (1, 2, 3))
    moved = moved + tuple(turn(bottom[k], "y", k) for k in (1, 2, 3))
    moved, ffn_grads = tied((moved, ffn_grads))

    grad_rows = lax.dynamic_slice_in_dim(
        out_cotangent.reshape(count, width), place * own, own, axis=0
    )
    block_rows, d_residual, d_low, second_part, d_mixer, edges = residual_back(
        (top[0], bottom[0]),
        moved,
        residual,
        inverse_two,
        second_gain.reshape(1, width),
        grad_rows,
        out_all,
        gates[1, :8],
        rows_one,
        rows_two,
    )
    block_output = lax.all_gather(block_rows, TP, axis=0, tiled=True)
    pairs = []
    for sq in range(8):
        for j in range(TPS):
            if j % per_seq:
                pairs.append((sq * TPS + j, sq * TPS + j - 1))
            elif sq:
                pairs.append((sq * TPS + j, (sq - 1) * TPS + j + per_seq - 1))
    edges = lax.ppermute(edges, ALL, pairs)
    out_part = dot(mixer, d_low, 1, 0, bf16).reshape(TPS, 2, chans // 2, width)
    theirs = swap_cores(jnp.where(is_low, out_part[:, 1], out_part[:, 0]))
    out_part = jnp.where(is_low, out_part[:, 0], out_part[:, 1]).astype(f32) + theirs.astype(f32)
    input_rows, exchanged = mixer_back(
        d_mixer,
        edges,
        gates,
        lags,
        conv,
        rows_one,
        rows_two,
        taps,
        in_all,
        rows_in,
        first_gain.reshape(1, width),
        d_residual,
        second_part,
        out_part.astype(bf16),
    )
    middle = 3 * chans // 2

    def exchange(early):
        exchanged, ffn_grads = early
        exchanged = lax.all_to_all(exchanged, TP, 0, 0, tiled=True)
        return exchanged, lax.all_gather(ffn_grads, SEQ, axis=0, tiled=True)

    input_first, input_last, exchanged, ffn_grads, block_output = plane_gather(
        input_rows, (exchanged, ffn_grads), exchange, block_output
    )
    received = exchanged[:, : 3 * chans].transpose(1, 0, 2)
    in_part = dot(received.reshape(3 * chans, count), normed1, 1, 0, bf16)
    small = jnp.sum(exchanged[:, 3 * chans :].astype(f32), axis=0).astype(bf16)
    out_part = small[24:].reshape(width // own, chans // 2, own).transpose(1, 0, 2)
    out_part = out_part.reshape(chans // 2, width)
    small = jnp.pad(small[:24].reshape(3, width), ((0, 5), (0, 0)))
    theirs = swap_cores(
        jnp.concatenate([jnp.where(is_low, in_part[middle:], in_part[:middle]), small], axis=0)
    )
    mine = jnp.where(is_low, in_part[:middle], in_part[middle:])
    mine = jnp.concatenate([mine, small], axis=0).astype(f32) + theirs.astype(f32)
    mine = jnp.concatenate([mine.astype(bf16), out_part], axis=0)
    by_z = jnp.broadcast_to(mine[None], (RING,) + mine.shape)
    by_z = lax.all_to_all(by_z, "z", 0, 0, tiled=True)
    block_output = block_output.astype(f32)
    gate_grad = ffn_grads[:ff].astype(f32).T
    up_grad = ffn_grads[ff : 2 * ff].astype(f32).T
    down_grad = ffn_grads[2 * ff : 3 * ff].astype(f32)
    input_grad = absolute_rows(input_first + input_last, starts)

    by_z = by_z.astype(f32)
    total = (by_z[0] + by_z[2]) + (by_z[1] + by_z[3])
    small = total[middle : middle + 8]
    mine = jnp.concatenate([total[:middle], total[middle + 8 :]], axis=0).astype(bf16)
    theirs = swap_cores(mine)
    low, high = jnp.where(is_low, mine, theirs), jnp.where(is_low, theirs, mine)
    low, high = low.astype(f32), high.astype(f32)
    in_grad = jnp.concatenate([low[:middle], high[:middle]], axis=0)
    in_grad = in_grad.reshape(3, chans, width).transpose(2, 0, 1)
    out_grad = jnp.concatenate([low[middle:], high[middle:]], axis=0)
    first_grad, second_grad = small[0], small[1]
    taps_grad = small[2].reshape(8, own)[:3]
    taps_grad = lax.dynamic_slice_in_dim(taps_grad, place % 2 * chans, chans, axis=1)

    return (
        block_output.reshape(seqs, seg, width),
        input_grad.reshape(seqs, seg, width),
        first_grad,
        in_grad,
        taps_grad,
        out_grad,
        second_grad,
        gate_grad,
        up_grad,
        down_grad,
    )


def solution(mesh):
    grid = Mesh(mesh.devices.reshape(4, 2, RING, RING), ALL)
    return jax.shard_map(
        shards,
        mesh=grid,
        in_specs=(
            P(None, SEQ, None),
            P(),
            P(None, None, TP),
            P(None, TP),
            P(TP, None),
            P(),
            P(None, TP),
            P(None, TP),
            P(TP, None),
            P(),
            P(None, SEQ, None),
        ),
        out_specs=(
            P(None, SEQ, None),
            P(None, SEQ, None),
            P(),
            P(None, None, TP),
            P(None, TP),
            P(TP, None),
            P(),
            P(None, TP),
            P(None, TP),
            P(TP, None),
        ),
        check_vma=False,
    )
```

profile of v0, /device:TPU:65, one launch (start us, length us, event | category | flops | bytes accessed | tf_op | source)
XLA Modules:
  0.0 333.7 jit_solution(13318814469053904080)
XLA Ops:
  11.6 6.8 %all-to-all-start = ((bf16[16,32,1024]{2,1,0:T(8,128)(2,1)}), bf16[16,32,1024]{2,1,0:T(8,128)(2,1)}, u32[]{:S(2)}, u32[]{:S(2)}) async-start(bf16[16,32,1024]{2,1,0:T(8,128)(2,1)} %broadcast_in_dim.10), calls=%async_computation | async-start | bytes 2097152 | tf_op jit(solution)/shard_map/all_to_all | solution.py:661
  18.4 3.4 %copy-done.3 = f32[2,1024,1024]{2,1,0:T(8,128)S(1)} copy-done((f32[2,1024,1024]{2,1,0:T(8,128)S(1)}, f32[2,1024,1024]{2,1,0:T(8,128)}, u32[]{:S(2)}) %copy-start.3) | copy-done | bytes 8388632
  21.8 4.6 %norm_and_project.1 = (bf16[2048,1024]{1,0:T(8,128)(2,1)}, f32[192,2048]{1,0:T(8,128)S(1)}) custom-call(f32[2048,1024]{1,0:T(8,128)S(1)} %bitcast.166, f32[1,1024]{1,0:T(1,128)S(1)} %bitcast.172, bf16[192,1024]{1,0:T(8,128)(2,1)S(1)} %bitcast.169), custom_call_target="tpu_custom_call" | custom-call | flops 805306368 | bytes 12582912 | tf_op jit(solution)/shard_map/norm_and_project/pallas_call | solution.py:381
  27.1 4.1 %collective-permute-start = (bf16[2,8,1024]{2,1,0:T(8,128)(2,1)S(1)}, bf16[2,8,1024]{2,1,0:T(8,128)(2,1)S(1)}, u32[]{:S(2)}, u32[]{:S(2)}) collective-permute-start(bf16[2,8,1024]{2,1,0:T(8,128)(2,1)S(1)} %slice.266), channel_id=1, source_target_pairs={{0,16},{1,17},{2,18},{3,19},{4,20},{5,21},{6,22},{7,23},{8,24},{9,... | collective-permute-start | bytes 98312 | tf_op jit(solution)/shard_map/ppermute | solution.py:687
  33.2 1.6 all-to-all-done
  34.7 2.5 collective-permute-start.1
  38.6 3.7 %all-to-all-start.1 = ((bf16[16,64,128]{2,1,0:T(8,128)(2,1)}), bf16[16,64,128]{2,1,0:T(8,128)(2,1)S(1)}, u32[]{:S(2)}, u32[]{:S(2)}) async-start(bf16[16,64,128]{2,1,0:T(8,128)(2,1)} %pad_maximum_fusion.4), calls=%async_computation.1 | async-start | bytes 524288 | tf_op jit(solution)/shard_map/all_to_all | solution.py:705
  42.3 1.7 select_bitcast_fusion.2
  44.3 6.5 %all-to-all-done.1 = bf16[16,64,128]{2,1,0:T(8,128)(2,1)S(1)} async-done(((bf16[16,64,128]{2,1,0:T(8,128)(2,1)}), bf16[16,64,128]{2,1,0:T(8,128)(2,1)S(1)}, u32[]{:S(2)}, u32[]{:S(2)}) %all-to-all-start.1) | async-done | bytes 262176 | tf_op jit(solution)/shard_map/all_to_all | solution.py:705
  51.5 1.6 multiply_reduce_fusion
  53.7 1.8 collective-permute-start.3
  57.0 1.7 collective-permute-done.2.refs_2_
  58.6 1.7 collective-permute-done.3.refs_3_
  60.4 4.2 %collective-permute-done.4.refs_4_ = bf16[64,1024]{1,0:T(8,128)(2,1)S(1)} collective-permute-done((bf16[64,1024]{1,0:T(8,128)(2,1)S(1)}, bf16[64,1024]{1,0:T(8,128)(2,1)S(1)}, u32[]{:S(2)}, u32[]{:S(2)}) %collective-permute-start.4) | collective-permute-done | bytes 131104 | tf_op jit(solution)/shard_map/ppermute | solution.py:20
  68.4 1.7 collective-permute-start.9
  71.4 3.4 %copy-done.4 = f32[2,1024,1024]{2,1,0:T(8,128)S(1)} copy-done((f32[2,1024,1024]{2,1,0:T(8,128)S(1)}, f32[2,1024,1024]{2,1,0:T(8,128)}, u32[]{:S(2)}) %copy-start.4) | copy-done | bytes 8388632
  74.8 7.9 %relative_rows.1 = (bf16[1536,1024]{1,0:T(8,128)(2,1)S(1)}, bf16[512,1024]{1,0:T(8,128)(2,1)S(1)}, f32[1536,288]{1,0:T(8,128)S(1)}, f32[512,288]{1,0:T(8,128)S(1)}) custom-call(s32[32]{0:T(128)S(1)} %get-tuple-element.307.table, f32[2048,1024]{1,0:T(8,128)S(1)} %bitcast.168, bf16[288,1024]{1,0:T(8,128)(2,1)S(1)} %copy-done.19), custom_call_target="tpu_custom_call" | custom-call | flops 1207959552 | bytes 12582912 | tf_op jit(solution)/shard_map/relative_rows/pallas_call | solution.py:292
  83.7 4.1 %collective-permute-done.11.refs_3_.refs_5_ = bf16[256,1024]{1,0:T(8,128)(2,1)S(1)} collective-permute-done((bf16[256,1024]{1,0:T(8,128)(2,1)S(1)}, bf16[256,1024]{1,0:T(8,128)(2,1)S(1)}, u32[]{:S(2)}, u32[]{:S(2)}) %collective-permute-start.11) | collective-permute-done | bytes 524320 | tf_op jit(solution)/shard_map/ppermute | solution.py:20
  87.7 4.1 %collective-permute-done.9.refs_1_.refs_2_ = bf16[256,1024]{1,0:T(8,128)(2,1)S(1)} collective-permute-done((bf16[256,1024]{1,0:T(8,128)(2,1)S(1)}, bf16[256,1024]{1,0:T(8,128)(2,1)S(1)}, u32[]{:S(2)}, u32[]{:S(2)}) %collective-permute-start.9) | collective-permute-done | bytes 524320 | tf_op jit(solution)/shard_map/ppermute | solution.py:20
  92.0 1.7 collective-permute-start.12
  94.7 2.9 collective-permute-start.15
  97.6 10.6 %feed_forward.2 = (bf16[256,2048]{1,0:T(8,128)(2,1)S(1)}, bf16[256,2048]{1,0:T(8,128)(2,1)}, bf16[256,2048]{1,0:T(8,128)(2,1)}, bf16[256,2048]{1,0:T(8,128)(2,1)...) custom-call(bf16[256,1024]{1,0:T(8,128)(2,1)S(1)} %get-tuple-element, ...), custom_call_target="tpu_custom_call" | custom-call | flops 4529848320 | bytes 9437184 | tf_op jit(solution)/shard_map/feed_forward/pallas_call | solution.py:596
  109.4 3.3 feed_forward.3
  113.1 2.3 collective-permute-start.17
  115.5 2.9 collective-permute-start.19
  118.4 4.3 %collective-permute-done.16.refs_4_ = bf16[128,2048]{1,0:T(8,128)(2,1)S(1)} collective-permute-done((bf16[128,2048]{1,0:T(8,128)(2,1)S(1)}, bf16[128,2048]{1,0:T(8,128)(2,1)S(1)}, u32[]{:S(2)}, u32[]{:S(2)}) %collective-permute-start.16) | collective-permute-done | bytes 524320 | tf_op jit(solution)/shard_map/ppermute | solution.py:20
  122.7 2.3 collective-permute-done.18.refs_6_
  130.3 1.6 maximum_maximum_fusion
  132.0 2.6 add_halves.1
  134.7 2.7 collective-permute-start.21
  137.3 2.9 collective-permute-start.23
  142.8 3.5 %slice.285 = bf16[8,16,3,8,1024]{4,3,2,1,0:T(8,128)(2,1)S(1)} slice(bf16[8,16,4,8,1024]{4,3,2,1,0:T(8,128)(2,1)} %bitcast.183), slice={[0:8], [0:16], [0:3], [0:8], [0:1024]} | slice | bytes 12582912 | tf_op jit(solution)/shard_map/slice | solution.py:676
  147.3 3.4 %copy.80 = bf16[8,16,3,8,1024]{4,3,0,1,2:T(8,128)(2,1)} copy(bf16[8,16,3,8,1024]{4,3,2,1,0:T(8,128)(2,1)S(1)} %slice.285) | data formatting | bytes 12582912
  151.0 2.9 copy-done.2
  153.8 2.4 mixer_gates.1
  157.1 2.6 ring_sums.3
  161.6 1.5 collective-permute-start.29
  163.1 2.5 ring_sums.2
  167.1 3.1 collective-permute-start.25
  172.2 1.9 constant_dynamic-slice_fusion.refs_11_
  175.4 1.6 collective-permute-done.25.refs_3_
  177.3 5.0 %residual_back.1 = (bf16[128,1024]{1,0:T(8,128)(2,1)}, f32[128,1024]{1,0:T(8,128)}, bf16[128,1024]{1,0:T(8,128)(2,1)}, f32[1,1024]{1,0:T(1,128)}, f32[128,1024]{1,0:T(8,128)}, /*index=5*/f32[16,1024]{1,0:T(8,128)}) custom-call(f32[64,2048]{1,0:T(8,128)} %copy-done.21, f32[64,2048]{1,0:T(8,128)} %copy-done.20, ...), custom_call_target="tpu_custom_call" | custom-call | flops 268435456 | bytes 7448064 | tf_op jit(solution)/shard_map/residual_back/pallas_call | solution.py:190
  182.3 1.9 convolution_convert_fusion
  184.3 9.0 %collective-permute-start.31 = (bf16[16,32,1024]{2,1,0:T(8,128)(2,1)S(1)}, bf16[16,32,1024]{2,1,0:T(8,128)(2,1)S(1)}, u32[]{:S(2)}, u32[]{:S(2)}) collective-permute-start(bf16[16,32,1024]{2,1,0:T(8,128)(2,1)S(1)} %select_bitcast_fusion), channel_id=1, source_target_pairs={{0,16},{16,0},{1,17},{17,1},{2,18},{18,2},{3,19},{19,3},{4,20},{20... | collective-permute-start | bytes 3145736 | tf_op jit(solution)/shard_map/ppermute | solution.py:237
  193.4 5.3 %collective-permute-start.30 = (f32[16,1024]{1,0:T(8,128)S(1)}, f32[16,1024]{1,0:T(8,128)S(1)}, u32[]{:S(2)}, u32[]{:S(2)}) collective-permute-start(f32[16,1024]{1,0:T(8,128)S(1)} %copy-done.39), channel_id=1, source_target_pairs={{1,0},{2,1},{3,2},{4,3},{5,4},{6,5},{7,6},{9,8},{10,9},{11,10},{12... | collective-permute-start | bytes 196616 | tf_op jit(solution)/shard_map/ppermute | solution.py:789
  200.6 1.7 mixer_back.1
  203.9 3.2 collective-permute-start.32
  207.8 2.7 collective-permute-start.35
  211.1 5.4 %collective-permute-start.37 = (bf16[64,1024]{1,0:T(8,128)(2,1)S(1)}, bf16[64,1024]{1,0:T(8,128)(2,1)S(1)}, u32[]{:S(2)}, u32[]{:S(2)}) collective-permute-start(bf16[64,1024]{1,0:T(8,128)(2,1)S(1)} %get-tuple-element.273.refs_1_), channel_id=1, source_target_pairs={{0,4},{4,8},{8,12},{12,0},{1,5},{5,9},{9,13},{13,1},{2,6},{6,10},{... | collective-permute-start | bytes 393224 | tf_op jit(solution)/shard_map/ppermute | solution.py:20
  216.5 1.7 collective-permute-done.34.refs_4_
  218.2 2.2 collective-permute-done.37.refs_7_
  220.4 7.4 %all-to-all-start.2 = ((bf16[16,472,128]{2,1,0:T(8,128)(2,1)}), bf16[16,472,128]{2,1,0:T(8,128)(2,1)}, u32[]{:S(2)}, u32[]{:S(2)}) async-start(bf16[16,472,128]{2,1,0:T(8,128)(2,1)} %copy-done.6), calls=%async_computation.3 | async-start | bytes 3866624 | tf_op jit(solution)/shard_map/all_to_all | solution.py:813
  229.8 2.6 collective-permute-start.38
  232.4 2.4 collective-permute-start.40
  234.8 43.5 %collective-permute-done.38.refs_0_.refs_1_ = bf16[256,1024]{1,0:T(8,128)(2,1)S(1)} collective-permute-done((bf16[256,1024]{1,0:T(8,128)(2,1)S(1)}, bf16[256,1024]{1,0:T(8,128)(2,1)S(1)}, u32[]{:S(2)}, u32[]{:S(2)}) %collective-permute-start.38) | collective-permute-done | bytes 524320 | tf_op jit(solution)/shard_map/ppermute | solution.py:20
  278.3 2.2 collective-permute-done.40.refs_2_.refs_4_
  282.0 3.4 %convolution_convert_fusion.1 = bf16[192,1024]{1,0:T(8,128)(2,1)S(1)} fusion(bf16[2048,1024]{1,0:T(8,128)(2,1)} %get-tuple-element.158, bf16[16,472,128]{2,1,0:T(8,128)(2,1)} %all-to-all-done.2), kind=kOutput, calls=%fused_computation.11 | convolution fusion | flops 805502976 | bytes 5373952 | tf_op jit(solution)/shard_map/dot_general | solution.py:615
  288.7 4.3 %all-to-all-start.3 = ((bf16[4,136,1024]{2,1,0:T(8,128)(2,1)}), bf16[4,136,1024]{2,1,0:T(8,128)(2,1)}, u32[]{:S(2)}, u32[]{:S(2)}) async-start(bf16[4,136,1024]{2,1,0:T(8,128)(2,1)} %broadcast_in_dim.14), calls=%async_computation.4 | async-start | bytes 2228224 | tf_op jit(solution)/shard_map/all_to_all | solution.py:832
  294.3 2.4 collective-permute-start.43
  297.6 3.4 %collective-permute-start.45 = (bf16[128,1024]{1,0:T(8,128)(2,1)}, bf16[128,1024]{1,0:T(8,128)(2,1)}, u32[]{:S(2)}, u32[]{:S(2)}) collective-permute-start(bf16[128,1024]{1,0:T(8,128)(2,1)} %get-tuple-element.294), channel_id=1, source_target_pairs={{0,3},{1,0},{2,1},{3,2},{4,7},{5,4},{6,5},{7,6},{8,11},{9,8},{10,9... | collective-permute-start | bytes 786440 | tf_op jit(solution)/shard_map/ppermute | solution.py:20
  301.0 6.7 %convert.33 = f32[2,1024,1024]{2,1,0:T(8,128)} convert(bf16[2,1024,1024]{2,1,0:T(8,128)(2,1)} %bitcast.185) | non-fusion elementwise | flops 2097152 | bytes 12582912 | tf_op jit(solution)/shard_map/reshape | solution.py:854
  307.7 5.9 %all-gather.7.cloned.1.call-done = bf16[896,1024]{1,0:T(8,128)(2,1)} async-done(((bf16[112,1024]{1,0:T(8,128)(2,1)}), bf16[896,1024]{1,0:T(8,128)(2,1)}) %all-gather.7.cloned.1.call-update) | async-done | bytes 1835024 | tf_op jit(solution)/shard_map/all_gather | solution.py:814
  313.6 5.1 %absolute_rows.1 = f32[2048,1024]{1,0:T(8,128)} custom-call(s32[32]{0:T(128)S(1)} %get-tuple-element.308.table, bf16[256,1024]{1,0:T(8,128)(2,1)S(1)} %get-tuple-element.282.refs_0_, bf16[256,1024]{1,0:T(8,128)(2,1)S(1)} %collective-permute-done.38.refs_0_.refs_1_, bf16[256,1024]{1,0:T(8,128)(2,1)S(1)} %collective-permute-done.39.refs_1_.refs_2_, ...), custom_call_target="tpu_custom_call" | custom-call | flops 2097152 | bytes 12582912 | tf_op jit(solution)/shard_map/absolute_rows/pallas_call | solution.py:348
  318.7 1.9 slice_convert_fusion
  (251 shorter events, 54.5 us)
Async XLA Ops:
  8.0 134.8 %all-gather.9.cloned.1.call-start = ((), (), s32[]{:S(2)}) async-start(), calls=%async_computation.8 | async-start | bytes 8454144 | tf_op jit(solution)/shard_map/all_gather | solution.py:671
  11.6 23.2 %all-to-all-start = ((bf16[16,32,1024]{2,1,0:T(8,128)(2,1)}), bf16[16,32,1024]{2,1,0:T(8,128)(2,1)}, u32[]{:S(2)}, u32[]{:S(2)}) async-start(bf16[16,32,1024]{2,1,0:T(8,128)(2,1)} %broadcast_in_dim.10), calls=%async_computation | async-start | bytes 2097152 | tf_op jit(solution)/shard_map/all_to_all | solution.py:661
  27.1 5.5 %collective-permute-start = (bf16[2,8,1024]{2,1,0:T(8,128)(2,1)S(1)}, bf16[2,8,1024]{2,1,0:T(8,128)(2,1)S(1)}, u32[]{:S(2)}, u32[]{:S(2)}) collective-permute-start(bf16[2,8,1024]{2,1,0:T(8,128)(2,1)S(1)} %slice.266), channel_id=1, source_target_pairs={{0,16},{1,17},{2,18},{3,19},{4,20},{5,21},{6,22},{7,23},{8,24},{9,... | collective-permute-start | bytes 98312 | tf_op jit(solution)/shard_map/ppermute | solution.py:687
  34.7 7.6 %collective-permute-start.1 = (bf16[16,32,1024]{2,1,0:T(8,128)(2,1)}, bf16[16,32,1024]{2,1,0:T(8,128)(2,1)}, u32[]{:S(2)}, u32[]{:S(2)}) collective-permute-start(bf16[16,32,1024]{2,1,0:T(8,128)(2,1)} %all-to-all-done), channel_id=1, source_target_pairs={{0,16},{16,0},{1,17},{17,1},{2,18},{18,2},{3,19},{19,3},{4,20},{20... | collective-permute-start | bytes 3145736 | tf_op jit(solution)/shard_map/ppermute | solution.py:237
  38.6 12.2 %all-to-all-start.1 = ((bf16[16,64,128]{2,1,0:T(8,128)(2,1)}), bf16[16,64,128]{2,1,0:T(8,128)(2,1)S(1)}, u32[]{:S(2)}, u32[]{:S(2)}) async-start(bf16[16,64,128]{2,1,0:T(8,128)(2,1)} %pad_maximum_fusion.4), calls=%async_computation.1 | async-start | bytes 524288 | tf_op jit(solution)/shard_map/all_to_all | solution.py:705
  42.3 133.1 %reduce-scatter.2.cloned.1.call-start = ((), (), s32[]{:S(2)}) async-start(), calls=%async_computation.5 | async-start | bytes 2064384 | tf_op jit(solution)/shard_map/reduce_scatter | solution.py:747
  51.5 19.8 %copy-start.36 = (s32[32]{0:T(128)S(1)}, s32[32]{0:T(128)}, u32[]{:S(2)}) copy-start(s32[32]{0:T(128)} %constant.117.clone) | copy-start | bytes 388
  51.5 19.8 %copy-start.37 = (s32[32]{0:T(128)S(1)}, s32[32]{0:T(128)}, u32[]{:S(2)}) copy-start(s32[32]{0:T(128)} %constant.125) | copy-start | bytes 388
  51.5 19.8 %copy-start.38 = (s32[32]{0:T(128)S(1)}, s32[32]{0:T(128)}, u32[]{:S(2)}) copy-start(s32[32]{0:T(128)} %constant.126) | copy-start | bytes 388
  51.5 19.8 %copy-start.19 = (bf16[288,1024]{1,0:T(8,128)(2,1)S(1)}, bf16[288,1024]{1,0:T(8,128)(2,1)}, u32[]{:S(2)}) copy-start(bf16[288,1024]{1,0:T(8,128)(2,1)} %refs_5_.1) | copy-start | bytes 1769476
  53.1 29.7 %copy-start.29 = (f32[128,1024]{1,0:T(8,128)}, f32[128,1024]{1,0:T(8,128)S(1)}, u32[]{:S(2)}) copy-start(f32[128,1024]{1,0:T(8,128)S(1)} %get-tuple-element.343.refs_8_) | copy-start | bytes 1572868
  53.6 5.0 %collective-permute-start.2 = (bf16[64,1024]{1,0:T(8,128)(2,1)S(1)}, bf16[64,1024]{1,0:T(8,128)(2,1)S(1)}, u32[]{:S(2)}, u32[]{:S(2)}) collective-permute-start(bf16[64,1024]{1,0:T(8,128)(2,1)S(1)} %get-tuple-element.160.refs_0_), channel_id=1, source_target_pairs={{0,3},{1,0},{2,1},{3,2},{4,7},{5,4},{6,5},{7,6},{8,11},{9,8},{10,9... | collective-permute-start | bytes 393224 | tf_op jit(solution)/shard_map/ppermute | solution.py:20
  53.7 6.7 %collective-permute-start.3 = (bf16[64,1024]{1,0:T(8,128)(2,1)S(1)}, bf16[64,1024]{1,0:T(8,128)(2,1)S(1)}, u32[]{:S(2)}, u32[]{:S(2)}) collective-permute-start(bf16[64,1024]{1,0:T(8,128)(2,1)S(1)} %get-tuple-element.160.refs_0_), channel_id=1, source_target_pairs={{0,2},{1,3},{2,0},{3,1},{4,6},{5,7},{6,4},{7,5},{8,10},{9,11},{10,... | collective-permute-start | bytes 393224 | tf_op jit(solution)/shard_map/ppermute | solution.py:20
  55.5 9.1 %collective-permute-start.4 = (bf16[64,1024]{1,0:T(8,128)(2,1)S(1)}, bf16[64,1024]{1,0:T(8,128)(2,1)S(1)}, u32[]{:S(2)}, u32[]{:S(2)}) collective-permute-start(bf16[64,1024]{1,0:T(8,128)(2,1)S(1)} %get-tuple-element.160.refs_0_), channel_id=1, source_target_pairs={{0,1},{1,2},{2,3},{3,0},{4,5},{5,6},{6,7},{7,4},{8,9},{9,10},{10,1... | collective-permute-start | bytes 393224 | tf_op jit(solution)/shard_map/ppermute | solution.py:20
  55.5 9.1 %collective-permute-start.5 = (bf16[64,1024]{1,0:T(8,128)(2,1)S(1)}, bf16[64,1024]{1,0:T(8,128)(2,1)S(1)}, u32[]{:S(2)}, u32[]{:S(2)}) collective-permute-start(bf16[64,1024]{1,0:T(8,128)(2,1)S(1)} %get-tuple-element.161.refs_1_), channel_id=1, source_target_pairs={{0,12},{4,0},{8,4},{12,8},{1,13},{5,1},{9,5},{13,9},{2,14},{6,2},{... | collective-permute-start | bytes 393224 | tf_op jit(solution)/shard_map/ppermute | solution.py:20
  56.1 8.5 %collective-permute-start.6 = (bf16[64,1024]{1,0:T(8,128)(2,1)S(1)}, bf16[64,1024]{1,0:T(8,128)(2,1)S(1)}, u32[]{:S(2)}, u32[]{:S(2)}) collective-permute-start(bf16[64,1024]{1,0:T(8,128)(2,1)S(1)} %get-tuple-element.161.refs_1_), channel_id=1, source_target_pairs={{0,8},{4,12},{8,0},{12,4},{1,9},{5,13},{9,1},{13,5},{2,10},{6,14},... | collective-permute-start | bytes 393224 | tf_op jit(solution)/shard_map/ppermute | solution.py:20
  58.6 6.6 %collective-permute-start.7 = (bf16[64,1024]{1,0:T(8,128)(2,1)S(1)}, bf16[64,1024]{1,0:T(8,128)(2,1)S(1)}, u32[]{:S(2)}, u32[]{:S(2)}) collective-permute-start(bf16[64,1024]{1,0:T(8,128)(2,1)S(1)} %get-tuple-element.161.refs_1_), channel_id=1, source_target_pairs={{0,4},{4,8},{8,12},{12,0},{1,5},{5,9},{9,13},{13,1},{2,6},{6,10},{... | collective-permute-start | bytes 393224 | tf_op jit(solution)/shard_map/ppermute | solution.py:20
  66.6 17.0 %collective-permute-start.10 = (bf16[256,1024]{1,0:T(8,128)(2,1)S(1)}, bf16[256,1024]{1,0:T(8,128)(2,1)S(1)}, u32[]{:S(2)}, u32[]{:S(2)}) collective-permute-start(bf16[256,1024]{1,0:T(8,128)(2,1)S(1)} %get-tuple-element.243.refs_3_), channel_id=1, source_target_pairs={{0,3},{1,0},{2,1},{3,2},{4,7},{5,4},{6,5},{7,6},{8,11},{9,8},{10,9... | collective-permute-start | bytes 1572872 | tf_op jit(solution)/shard_map/ppermute | solution.py:20
  67.8 20.0 %collective-permute-start.11 = (bf16[256,1024]{1,0:T(8,128)(2,1)S(1)}, bf16[256,1024]{1,0:T(8,128)(2,1)S(1)}, u32[]{:S(2)}, u32[]{:S(2)}) collective-permute-start(bf16[256,1024]{1,0:T(8,128)(2,1)S(1)} %get-tuple-element.243.refs_3_), channel_id=1, source_target_pairs={{0,1},{1,2},{2,3},{3,0},{4,5},{5,6},{6,7},{7,4},{8,9},{9,10},{10,1... | collective-permute-start | bytes 1572872 | tf_op jit(solution)/shard_map/ppermute | solution.py:20
  68.1 19.6 %collective-permute-start.8 = (bf16[256,1024]{1,0:T(8,128)(2,1)S(1)}, bf16[256,1024]{1,0:T(8,128)(2,1)S(1)}, u32[]{:S(2)}, u32[]{:S(2)}) collective-permute-start(bf16[256,1024]{1,0:T(8,128)(2,1)S(1)} %get-tuple-element.240.refs_0_), channel_id=1, source_target_pairs={{0,12},{4,0},{8,4},{12,8},{1,13},{5,1},{9,5},{13,9},{2,14},{6,2},{... | collective-permute-start | bytes 1572872 | tf_op jit(solution)/shard_map/ppermute | solution.py:20
  68.4 23.4 %collective-permute-start.9 = (bf16[256,1024]{1,0:T(8,128)(2,1)S(1)}, bf16[256,1024]{1,0:T(8,128)(2,1)S(1)}, u32[]{:S(2)}, u32[]{:S(2)}) collective-permute-start(bf16[256,1024]{1,0:T(8,128)(2,1)S(1)} %get-tuple-element.240.refs_0_), channel_id=1, source_target_pairs={{0,4},{4,8},{8,12},{12,0},{1,5},{5,9},{9,13},{13,1},{2,6},{6,10},{... | collective-permute-start | bytes 1572872 | tf_op jit(solution)/shard_map/ppermute | solution.py:20
  92.0 17.3 %collective-permute-start.12 = (bf16[128,1024]{1,0:T(8,128)(2,1)S(1)}, bf16[128,1024]{1,0:T(8,128)(2,1)S(1)}, u32[]{:S(2)}, u32[]{:S(2)}) collective-permute-start(bf16[128,1024]{1,0:T(8,128)(2,1)S(1)} %get-tuple-element.176), channel_id=1, source_target_pairs={{0,4},{4,8},{8,12},{12,0},{1,5},{5,9},{9,13},{13,1},{2,6},{6,10},{... | collective-permute-start | bytes 786440 | tf_op jit(solution)/shard_map/ppermute | solution.py:20
  93.7 15.6 %collective-permute-start.13 = (bf16[128,1024]{1,0:T(8,128)(2,1)S(1)}, bf16[128,1024]{1,0:T(8,128)(2,1)S(1)}, u32[]{:S(2)}, u32[]{:S(2)}) collective-permute-start(bf16[128,1024]{1,0:T(8,128)(2,1)S(1)} %get-tuple-element.177), channel_id=1, source_target_pairs={{0,12},{4,0},{8,4},{12,8},{1,13},{5,1},{9,5},{13,9},{2,14},{6,2},{... | collective-permute-start | bytes 786440 | tf_op jit(solution)/shard_map/ppermute | solution.py:20
  94.7 14.6 %collective-permute-start.14 = (bf16[128,1024]{1,0:T(8,128)(2,1)S(1)}, bf16[128,1024]{1,0:T(8,128)(2,1)S(1)}, u32[]{:S(2)}, u32[]{:S(2)}) collective-permute-start(bf16[128,1024]{1,0:T(8,128)(2,1)S(1)} %get-tuple-element.178), channel_id=1, source_target_pairs={{0,1},{1,2},{2,3},{3,0},{4,5},{5,6},{6,7},{7,4},{8,9},{9,10},{10,1... | collective-permute-start | bytes 786440 | tf_op jit(solution)/shard_map/ppermute | solution.py:20
  94.7 14.6 %collective-permute-start.15 = (bf16[128,1024]{1,0:T(8,128)(2,1)S(1)}, bf16[128,1024]{1,0:T(8,128)(2,1)S(1)}, u32[]{:S(2)}, u32[]{:S(2)}) collective-permute-start(bf16[128,1024]{1,0:T(8,128)(2,1)S(1)} %get-tuple-element.179), channel_id=1, source_target_pairs={{0,3},{1,0},{2,1},{3,2},{4,7},{5,4},{6,5},{7,6},{8,11},{9,8},{10,9... | collective-permute-start | bytes 786440 | tf_op jit(solution)/shard_map/ppermute | solution.py:20
  112.7 10.0 %collective-permute-start.16 = (bf16[128,2048]{1,0:T(8,128)(2,1)S(1)}, bf16[128,2048]{1,0:T(8,128)(2,1)S(1)}, u32[]{:S(2)}, u32[]{:S(2)}) collective-permute-start(bf16[128,2048]{1,0:T(8,128)(2,1)S(1)} %get-tuple-element.201), channel_id=1, source_target_pairs={{0,4},{4,8},{8,12},{12,0},{1,5},{5,9},{9,13},{13,1},{2,6},{6,10},{... | collective-permute-start | bytes 1572872 | tf_op jit(solution)/shard_map/ppermute | solution.py:20
  113.1 9.6 %collective-permute-start.17 = (bf16[128,2048]{1,0:T(8,128)(2,1)S(1)}, bf16[128,2048]{1,0:T(8,128)(2,1)S(1)}, u32[]{:S(2)}, u32[]{:S(2)}) collective-permute-start(bf16[128,2048]{1,0:T(8,128)(2,1)S(1)} %get-tuple-element.202), channel_id=1, source_target_pairs={{0,12},{4,0},{8,4},{12,8},{1,13},{5,1},{9,5},{13,9},{2,14},{6,2},{... | collective-permute-start | bytes 1572872 | tf_op jit(solution)/shard_map/ppermute | solution.py:20
  115.5 9.5 %collective-permute-start.18 = (bf16[128,2048]{1,0:T(8,128)(2,1)S(1)}, bf16[128,2048]{1,0:T(8,128)(2,1)S(1)}, u32[]{:S(2)}, u32[]{:S(2)}) collective-permute-start(bf16[128,2048]{1,0:T(8,128)(2,1)S(1)} %get-tuple-element.203), channel_id=1, source_target_pairs={{0,1},{1,2},{2,3},{3,0},{4,5},{5,6},{6,7},{7,4},{8,9},{9,10},{10,1... | collective-permute-start | bytes 1572872 | tf_op jit(solution)/shard_map/ppermute | solution.py:20
  115.5 9.5 %collective-permute-start.19 = (bf16[128,2048]{1,0:T(8,128)(2,1)S(1)}, bf16[128,2048]{1,0:T(8,128)(2,1)S(1)}, u32[]{:S(2)}, u32[]{:S(2)}) collective-permute-start(bf16[128,2048]{1,0:T(8,128)(2,1)S(1)} %get-tuple-element.204), channel_id=1, source_target_pairs={{0,3},{1,0},{2,1},{3,2},{4,7},{5,4},{6,5},{7,6},{8,11},{9,8},{10,9... | collective-permute-start | bytes 1572872 | tf_op jit(solution)/shard_map/ppermute | solution.py:20
  131.9 148.6 %all-gather.5.cloned.1.call-start = ((), (), s32[]{:S(2)}) async-start(), calls=%async_computation.6 | async-start | bytes 4456448 | tf_op jit(solution)/shard_map/all_gather | solution.py:781
  134.6 21.7 %collective-permute-start.20 = (bf16[256,2048]{1,0:T(8,128)(2,1)}, bf16[256,2048]{1,0:T(8,128)(2,1)}, u32[]{:S(2)}, u32[]{:S(2)}) collective-permute-start(bf16[256,2048]{1,0:T(8,128)(2,1)} %get-tuple-element.219), channel_id=1, source_target_pairs={{0,4},{4,8},{8,12},{12,0},{1,5},{5,9},{9,13},{13,1},{2,6},{6,10},{... | collective-permute-start | bytes 3145736 | tf_op jit(solution)/shard_map/ppermute | solution.py:20
  134.7 21.6 %collective-permute-start.21 = (bf16[256,2048]{1,0:T(8,128)(2,1)}, bf16[256,2048]{1,0:T(8,128)(2,1)}, u32[]{:S(2)}, u32[]{:S(2)}) collective-permute-start(bf16[256,2048]{1,0:T(8,128)(2,1)} %get-tuple-element.220), channel_id=1, source_target_pairs={{0,12},{4,0},{8,4},{12,8},{1,13},{5,1},{9,5},{13,9},{2,14},{6,2},{... | collective-permute-start | bytes 3145736 | tf_op jit(solution)/shard_map/ppermute | solution.py:20
  137.3 19.7 %collective-permute-start.22 = (bf16[256,2048]{1,0:T(8,128)(2,1)}, bf16[256,2048]{1,0:T(8,128)(2,1)}, u32[]{:S(2)}, u32[]{:S(2)}) collective-permute-start(bf16[256,2048]{1,0:T(8,128)(2,1)} %get-tuple-element.221), channel_id=1, source_target_pairs={{0,1},{1,2},{2,3},{3,0},{4,5},{5,6},{6,7},{7,4},{8,9},{9,10},{10,1... | collective-permute-start | bytes 3145736 | tf_op jit(solution)/shard_map/ppermute | solution.py:20
  137.3 19.7 %collective-permute-start.23 = (bf16[256,2048]{1,0:T(8,128)(2,1)}, bf16[256,2048]{1,0:T(8,128)(2,1)}, u32[]{:S(2)}, u32[]{:S(2)}) collective-permute-start(bf16[256,2048]{1,0:T(8,128)(2,1)} %get-tuple-element.222), channel_id=1, source_target_pairs={{0,3},{1,0},{2,1},{3,2},{4,7},{5,4},{6,5},{7,6},{8,11},{9,8},{10,9... | collective-permute-start | bytes 3145736 | tf_op jit(solution)/shard_map/ppermute | solution.py:20
  156.2 18.6 %copy-start.7 = (f32[3,128,1024]{2,1,0:T(8,128)}, f32[3,128,1024]{2,1,0:T(8,128)S(1)}, u32[]{:S(2)}) copy-start(f32[3,128,1024]{2,1,0:T(8,128)S(1)} %get-tuple-element.263.refs_2_) | copy-start | bytes 4718596
  160.4 9.7 %collective-permute-start.27 = (bf16[64,2048]{1,0:T(8,128)(2,1)S(1)}, bf16[64,2048]{1,0:T(8,128)(2,1)S(1)}, u32[]{:S(2)}, u32[]{:S(2)}) collective-permute-start(bf16[64,2048]{1,0:T(8,128)(2,1)S(1)} %get-tuple-element.236), channel_id=1, source_target_pairs={{0,4},{4,8},{8,12},{12,0},{1,5},{5,9},{9,13},{13,1},{2,6},{6,10},{... | collective-permute-start | bytes 786440 | tf_op jit(solution)/shard_map/ppermute | solution.py:20
  160.4 15.0 %collective-permute-start.28 = (bf16[64,2048]{1,0:T(8,128)(2,1)S(1)}, bf16[64,2048]{1,0:T(8,128)(2,1)}, u32[]{:S(2)}, u32[]{:S(2)}) collective-permute-start(bf16[64,2048]{1,0:T(8,128)(2,1)S(1)} %get-tuple-element.237), channel_id=1, source_target_pairs={{0,8},{4,12},{8,0},{12,4},{1,9},{5,13},{9,1},{13,5},{2,10},{6,14},... | collective-permute-start | bytes 786440 | tf_op jit(solution)/shard_map/ppermute | solution.py:20
  161.6 13.8 %collective-permute-start.29 = (bf16[64,2048]{1,0:T(8,128)(2,1)S(1)}, bf16[64,2048]{1,0:T(8,128)(2,1)}, u32[]{:S(2)}, u32[]{:S(2)}) collective-permute-start(bf16[64,2048]{1,0:T(8,128)(2,1)S(1)} %get-tuple-element.238), channel_id=1, source_target_pairs={{0,12},{4,0},{8,4},{12,8},{1,13},{5,1},{9,5},{13,9},{2,14},{6,2},{... | collective-permute-start | bytes 786440 | tf_op jit(solution)/shard_map/ppermute | solution.py:20
  166.5 8.9 %collective-permute-start.24 = (bf16[64,2048]{1,0:T(8,128)(2,1)}, bf16[64,2048]{1,0:T(8,128)(2,1)}, u32[]{:S(2)}, u32[]{:S(2)}) collective-permute-start(bf16[64,2048]{1,0:T(8,128)(2,1)} %get-tuple-element.233), channel_id=1, source_target_pairs={{0,1},{1,2},{2,3},{3,0},{4,5},{5,6},{6,7},{7,4},{8,9},{9,10},{10,1... | collective-permute-start | bytes 786440 | tf_op jit(solution)/shard_map/ppermute | solution.py:20
  167.1 10.0 %collective-permute-start.25 = (bf16[64,2048]{1,0:T(8,128)(2,1)}, bf16[64,2048]{1,0:T(8,128)(2,1)}, u32[]{:S(2)}, u32[]{:S(2)}) collective-permute-start(bf16[64,2048]{1,0:T(8,128)(2,1)} %get-tuple-element.234), channel_id=1, source_target_pairs={{0,2},{1,3},{2,0},{3,1},{4,6},{5,7},{6,4},{7,5},{8,10},{9,11},{10,... | collective-permute-start | bytes 786440 | tf_op jit(solution)/shard_map/ppermute | solution.py:20
  170.9 6.4 %collective-permute-start.26 = (bf16[64,2048]{1,0:T(8,128)(2,1)}, bf16[64,2048]{1,0:T(8,128)(2,1)}, u32[]{:S(2)}, u32[]{:S(2)}) collective-permute-start(bf16[64,2048]{1,0:T(8,128)(2,1)} %get-tuple-element.235), channel_id=1, source_target_pairs={{0,3},{1,0},{2,1},{3,2},{4,7},{5,4},{6,5},{7,6},{8,11},{9,8},{10,9... | collective-permute-start | bytes 786440 | tf_op jit(solution)/shard_map/ppermute | solution.py:20
  177.3 23.3 %slice-start = ((s8[6291456]{0:T(1024)(128)(4,1)}), s8[2097152]{0:T(1024)(128)(4,1)S(1)}, s32[]{:S(2)}) async-start(s8[6291456]{0:T(1024)(128)(4,1)} %bitcast.162), calls=%async_computation.9 | async-start | bytes 4194304
  182.3 18.2 %slice-start.1 = ((s8[6291456]{0:T(1024)(128)(4,1)}), s8[4194304]{0:T(1024)(128)(4,1)S(1)}, s32[]{:S(2)}) async-start(s8[6291456]{0:T(1024)(128)(4,1)} %bitcast.162), calls=%async_computation.10 | async-start | bytes 8388608
  184.3 14.4 %collective-permute-start.31 = (bf16[16,32,1024]{2,1,0:T(8,128)(2,1)S(1)}, bf16[16,32,1024]{2,1,0:T(8,128)(2,1)S(1)}, u32[]{:S(2)}, u32[]{:S(2)}) collective-permute-start(bf16[16,32,1024]{2,1,0:T(8,128)(2,1)S(1)} %select_bitcast_fusion), channel_id=1, source_target_pairs={{0,16},{16,0},{1,17},{17,1},{2,18},{18,2},{3,19},{19,3},{4,20},{20... | collective-permute-start | bytes 3145736 | tf_op jit(solution)/shard_map/ppermute | solution.py:237
  193.4 7.1 %collective-permute-start.30 = (f32[16,1024]{1,0:T(8,128)S(1)}, f32[16,1024]{1,0:T(8,128)S(1)}, u32[]{:S(2)}, u32[]{:S(2)}) collective-permute-start(f32[16,1024]{1,0:T(8,128)S(1)} %copy-done.39), channel_id=1, source_target_pairs={{1,0},{2,1},{3,2},{4,3},{5,4},{6,5},{7,6},{9,8},{10,9},{11,10},{12... | collective-permute-start | bytes 196616 | tf_op jit(solution)/shard_map/ppermute | solution.py:789
  203.9 7.2 %collective-permute-start.32 = (bf16[64,1024]{1,0:T(8,128)(2,1)S(1)}, bf16[64,1024]{1,0:T(8,128)(2,1)S(1)}, u32[]{:S(2)}, u32[]{:S(2)}) collective-permute-start(bf16[64,1024]{1,0:T(8,128)(2,1)S(1)} %get-tuple-element.272.refs_0_), channel_id=1, source_target_pairs={{0,3},{1,0},{2,1},{3,2},{4,7},{5,4},{6,5},{7,6},{8,11},{9,8},{10,9... | collective-permute-start | bytes 393224 | tf_op jit(solution)/shard_map/ppermute | solution.py:20
  207.1 9.4 %collective-permute-start.33 = (bf16[64,1024]{1,0:T(8,128)(2,1)S(1)}, bf16[64,1024]{1,0:T(8,128)(2,1)S(1)}, u32[]{:S(2)}, u32[]{:S(2)}) collective-permute-start(bf16[64,1024]{1,0:T(8,128)(2,1)S(1)} %get-tuple-element.272.refs_0_), channel_id=1, source_target_pairs={{0,2},{1,3},{2,0},{3,1},{4,6},{5,7},{6,4},{7,5},{8,10},{9,11},{10,... | collective-permute-start | bytes 393224 | tf_op jit(solution)/shard_map/ppermute | solution.py:20
  207.1 11.0 %collective-permute-start.34 = (bf16[64,1024]{1,0:T(8,128)(2,1)S(1)}, bf16[64,1024]{1,0:T(8,128)(2,1)S(1)}, u32[]{:S(2)}, u32[]{:S(2)}) collective-permute-start(bf16[64,1024]{1,0:T(8,128)(2,1)S(1)} %get-tuple-element.272.refs_0_), channel_id=1, source_target_pairs={{0,1},{1,2},{2,3},{3,0},{4,5},{5,6},{6,7},{7,4},{8,9},{9,10},{10,1... | collective-permute-start | bytes 393224 | tf_op jit(solution)/shard_map/ppermute | solution.py:20
  207.8 10.4 %collective-permute-start.35 = (bf16[64,1024]{1,0:T(8,128)(2,1)S(1)}, bf16[64,1024]{1,0:T(8,128)(2,1)S(1)}, u32[]{:S(2)}, u32[]{:S(2)}) collective-permute-start(bf16[64,1024]{1,0:T(8,128)(2,1)S(1)} %get-tuple-element.273.refs_1_), channel_id=1, source_target_pairs={{0,12},{4,0},{8,4},{12,8},{1,13},{5,1},{9,5},{13,9},{2,14},{6,2},{... | collective-permute-start | bytes 393224 | tf_op jit(solution)/shard_map/ppermute | solution.py:20
  210.4 7.7 %collective-permute-start.36 = (bf16[64,1024]{1,0:T(8,128)(2,1)S(1)}, bf16[64,1024]{1,0:T(8,128)(2,1)S(1)}, u32[]{:S(2)}, u32[]{:S(2)}) collective-permute-start(bf16[64,1024]{1,0:T(8,128)(2,1)S(1)} %get-tuple-element.273.refs_1_), channel_id=1, source_target_pairs={{0,8},{4,12},{8,0},{12,4},{1,9},{5,13},{9,1},{13,5},{2,10},{6,14},... | collective-permute-start | bytes 393224 | tf_op jit(solution)/shard_map/ppermute | solution.py:20
  211.1 9.3 %collective-permute-start.37 = (bf16[64,1024]{1,0:T(8,128)(2,1)S(1)}, bf16[64,1024]{1,0:T(8,128)(2,1)S(1)}, u32[]{:S(2)}, u32[]{:S(2)}) collective-permute-start(bf16[64,1024]{1,0:T(8,128)(2,1)S(1)} %get-tuple-element.273.refs_1_), channel_id=1, source_target_pairs={{0,4},{4,8},{8,12},{12,0},{1,5},{5,9},{9,13},{13,1},{2,6},{6,10},{... | collective-permute-start | bytes 393224 | tf_op jit(solution)/shard_map/ppermute | solution.py:20
  220.4 60.2 %all-to-all-start.2 = ((bf16[16,472,128]{2,1,0:T(8,128)(2,1)}), bf16[16,472,128]{2,1,0:T(8,128)(2,1)}, u32[]{:S(2)}, u32[]{:S(2)}) async-start(bf16[16,472,128]{2,1,0:T(8,128)(2,1)} %copy-done.6), calls=%async_computation.3 | async-start | bytes 3866624 | tf_op jit(solution)/shard_map/all_to_all | solution.py:813
  227.7 85.8 %all-gather.7.cloned.1.call-start = ((), (), s32[]{:S(2)}) async-start(), calls=%async_computation.7 | async-start | bytes 2064384 | tf_op jit(solution)/shard_map/all_gather | solution.py:814
  229.8 48.5 %collective-permute-start.38 = (bf16[256,1024]{1,0:T(8,128)(2,1)S(1)}, bf16[256,1024]{1,0:T(8,128)(2,1)S(1)}, u32[]{:S(2)}, u32[]{:S(2)}) collective-permute-start(bf16[256,1024]{1,0:T(8,128)(2,1)S(1)} %get-tuple-element.282.refs_0_), channel_id=1, source_target_pairs={{0,12},{4,0},{8,4},{12,8},{1,13},{5,1},{9,5},{13,9},{2,14},{6,2},{... | collective-permute-start | bytes 1572872 | tf_op jit(solution)/shard_map/ppermute | solution.py:20
  232.4 45.9 %collective-permute-start.39 = (bf16[256,1024]{1,0:T(8,128)(2,1)S(1)}, bf16[256,1024]{1,0:T(8,128)(2,1)S(1)}, u32[]{:S(2)}, u32[]{:S(2)}) collective-permute-start(bf16[256,1024]{1,0:T(8,128)(2,1)S(1)} %get-tuple-element.282.refs_0_), channel_id=1, source_target_pairs={{0,4},{4,8},{8,12},{12,0},{1,5},{5,9},{9,13},{13,1},{2,6},{6,10},{... | collective-permute-start | bytes 1572872 | tf_op jit(solution)/shard_map/ppermute | solution.py:20
  232.4 48.1 %collective-permute-start.40 = (bf16[256,1024]{1,0:T(8,128)(2,1)S(1)}, bf16[256,1024]{1,0:T(8,128)(2,1)S(1)}, u32[]{:S(2)}, u32[]{:S(2)}) collective-permute-start(bf16[256,1024]{1,0:T(8,128)(2,1)S(1)} %get-tuple-element.283.refs_3_), channel_id=1, source_target_pairs={{0,3},{1,0},{2,1},{3,2},{4,7},{5,4},{6,5},{7,6},{8,11},{9,8},{10,9... | collective-permute-start | bytes 1572872 | tf_op jit(solution)/shard_map/ppermute | solution.py:20
  234.8 45.7 %collective-permute-start.41 = (bf16[256,1024]{1,0:T(8,128)(2,1)S(1)}, bf16[256,1024]{1,0:T(8,128)(2,1)S(1)}, u32[]{:S(2)}, u32[]{:S(2)}) collective-permute-start(bf16[256,1024]{1,0:T(8,128)(2,1)S(1)} %get-tuple-element.283.refs_3_), channel_id=1, source_target_pairs={{0,1},{1,2},{2,3},{3,0},{4,5},{5,6},{6,7},{7,4},{8,9},{9,10},{10,1... | collective-permute-start | bytes 1572872 | tf_op jit(solution)/shard_map/ppermute | solution.py:20
  285.5 1.9 collective-permute-start.46
  288.7 32.0 %all-to-all-start.3 = ((bf16[4,136,1024]{2,1,0:T(8,128)(2,1)}), bf16[4,136,1024]{2,1,0:T(8,128)(2,1)}, u32[]{:S(2)}, u32[]{:S(2)}) async-start(bf16[4,136,1024]{2,1,0:T(8,128)(2,1)} %broadcast_in_dim.14), calls=%async_computation.4 | async-start | bytes 2228224 | tf_op jit(solution)/shard_map/all_to_all | solution.py:832
  293.9 19.6 %collective-permute-start.42 = (bf16[128,1024]{1,0:T(8,128)(2,1)}, bf16[128,1024]{1,0:T(8,128)(2,1)S(1)}, u32[]{:S(2)}, u32[]{:S(2)}) collective-permute-start(bf16[128,1024]{1,0:T(8,128)(2,1)} %get-tuple-element.291), channel_id=1, source_target_pairs={{0,4},{4,8},{8,12},{12,0},{1,5},{5,9},{9,13},{13,1},{2,6},{6,10},{... | collective-permute-start | bytes 786440 | tf_op jit(solution)/shard_map/ppermute | solution.py:20
  294.3 19.3 %collective-permute-start.43 = (bf16[128,1024]{1,0:T(8,128)(2,1)}, bf16[128,1024]{1,0:T(8,128)(2,1)}, u32[]{:S(2)}, u32[]{:S(2)}) collective-permute-start(bf16[128,1024]{1,0:T(8,128)(2,1)} %get-tuple-element.292), channel_id=1, source_target_pairs={{0,12},{4,0},{8,4},{12,8},{1,13},{5,1},{9,5},{13,9},{2,14},{6,2},{... | collective-permute-start | bytes 786440 | tf_op jit(solution)/shard_map/ppermute | solution.py:20
  296.7 16.9 %collective-permute-start.44 = (bf16[128,1024]{1,0:T(8,128)(2,1)}, bf16[128,1024]{1,0:T(8,128)(2,1)}, u32[]{:S(2)}, u32[]{:S(2)}) collective-permute-start(bf16[128,1024]{1,0:T(8,128)(2,1)} %get-tuple-element.293), channel_id=1, source_target_pairs={{0,1},{1,2},{2,3},{3,0},{4,5},{5,6},{6,7},{7,4},{8,9},{9,10},{10,1... | collective-permute-start | bytes 786440 | tf_op jit(solution)/shard_map/ppermute | solution.py:20
  297.6 16.0 %collective-permute-start.45 = (bf16[128,1024]{1,0:T(8,128)(2,1)}, bf16[128,1024]{1,0:T(8,128)(2,1)}, u32[]{:S(2)}, u32[]{:S(2)}) collective-permute-start(bf16[128,1024]{1,0:T(8,128)(2,1)} %get-tuple-element.294), channel_id=1, source_target_pairs={{0,3},{1,0},{2,1},{3,2},{4,7},{5,4},{6,5},{7,6},{8,11},{9,8},{10,9... | collective-permute-start | bytes 786440 | tf_op jit(solution)/shard_map/ppermute | solution.py:20
  322.4 1.6 collective-permute-start.47
  (34 other events, 223.2 us)
Sparse Core Ops, SparseCore 0:
  12.6 83.2 all-gather.8
Sparse Core Ops, SparseCore 1:
  132.0 34.8 reduce-scatter.1
  182.4 97.7 all-gather.4
  281.7 31.8 all-gather.6
where the time goes:
time: 339 us; the launch traced here: 334 us
  starting transfers between devices  100 us (29%)
  waiting for transfers between devices  93 us (27%)
  Pallas kernels  53.4 us (16%)
  local copies, waits for them, and re-layouts  35.2 us (10%)
  other arithmetic  21.8 us (6%)
  between operations  17.7 us (5%)
  matrix products  12.2 us (4%)
    ppermute x42, waiting for transfers between devices, turn(): lax.ppermute(value, axis, [(i, (i + steps) % RING) for i in range(RING)])  76.2 us
    ppermute x42, starting transfers between devices, turn(): lax.ppermute(value, axis, [(i, (i + steps) % RING) for i in range(RING)])  56.1 us
    unnamed x89, local copies, waits for them, and re-layouts  19.2 us
    pallas_call x2, Pallas kernels, feed_forward(): pl.pallas_call(body, in_specs=in_vmem(len(norms)) + [pl.BlockSpec(memory_...  13.9 us
    ppermute x4, starting transfers between devices, swap_cores(): return lax.ppermute(value, 'core', [(0, 1), (1, 0)])  12.7 us
    dot_general x11, matrix products, dot(): lax.dot_general(left, right, (((left_dim,), (right_dim,)), ((), ())), pre...  12.2 us
    pallas_call x1, Pallas kernels, relative_rows(): pl.pallas_call(body, grid_spec=pltpu.PrefetchScalarGridSpec(num_scalar_pr...  7.94 us
    all_to_all x1, starting transfers between devices, exchange(): exchanged = lax.all_to_all(exchanged, TP, 0, 0, tiled=True)  7.37 us
  transfers between devices with their start and end apart: 56, of which 21 were waited for; matrix products, arithmetic and copies ran while one was open for 14% of the time, Pallas kernels for 14%

commit v1 on v0

--- a/solution.py
+++ b/solution.py
@@ -35,7 +35,7 @@
 tied = lax.optimization_barrier
 
 
-def plane_gather(value, early=(), launch=None, beside=()):
+def plane_gather(value, early=(), launch=None, beside=(), own=None):
     half = value.shape[0] // 2
     top, bottom = assemble((value,), (((0, 0, half),), ((0, half, half),)))
     near = tuple(turn(top, "x", k) for k in (3, 2, 1)) + tuple(turn(bottom, "y", k) for k in (3, 2, 1))
@@ -49,10 +49,12 @@
         ),
     )
     near = ring_near(top, "y") + ring_near(bottom, "x")
+    if own:
+        beside = (beside, own([top, bottom]))
     near, launched, beside = tied((near, launched, beside))
     far = ring_far(near, ("y", "x"))
     far, beside_last = tied((far, beside_last))
-    return [top, near[0], near[1], bottom, near[2], near[3]], list(far), launched, beside_last, beside
+    return [top, bottom, *near], list(far), launched, beside_last, beside
 
 
 def assemble(sources, plans):
@@ -237,7 +239,7 @@
     return lax.ppermute(value, "core", [(0, 1), (1, 0)])
 
 
-CHUNKS = ((0, 0), (0, 1), (0, 3), (1, 0), (1, 1), (1, 3), (0, 2), (1, 2))
+CHUNKS = ((0, 0), (1, 0), (0, 1), (0, 3), (1, 1), (1, 3), (0, 2), (1, 2))
 
 
 def plane_starts(half):
@@ -557,8 +559,9 @@
     )(*operands)
 
 
-def feed_forward(norms, d_hidden, gate_t, up_t, down, pieces):
-    count, ff = d_hidden.shape
+def feed_forward(norms, d_hidden, start, gate_t, up_t, down, pieces):
+    ff = d_hidden.shape[1]
+    count = norms[0].shape[0] * len(norms)
     width = down.shape[1]
     step = norms[0].shape[0]
     piece = count // pieces
@@ -567,7 +570,7 @@
         norm_refs, rest = refs[: len(norms)], refs[len(norms) :]
         d_hbm, gate_ref, up_ref, down_ref = rest[:4]
         outs, (d_gate_ref, d_up_ref, hidden_ref, d_ref, sem) = rest[4:-5], rest[-5:]
-        load = pltpu.make_async_copy(d_hbm, d_ref, sem)
+        load = pltpu.make_async_copy(d_hbm.at[pl.ds(start, count)], d_ref, sem)
         load.start()
         for k, norm_ref in enumerate(norm_refs):
             part = slice(k * step, (k + 1) * step)
@@ -599,7 +602,7 @@
         out_specs=in_vmem(pieces + 3),
         out_shape=[jax.ShapeDtypeStruct((piece, 2 * width), bf16)] * pieces
         + [jax.ShapeDtypeStruct((count, ff), bf16)] * 3,
-        scratch_shapes=[pltpu.VMEM(d_hidden.shape, f32), pltpu.SemaphoreType.DMA(())],
+        scratch_shapes=[pltpu.VMEM((count, ff), f32), pltpu.SemaphoreType.DMA(())],
         compiler_params=pltpu.CompilerParams(vmem_limit_bytes=12 * 1024 * 1024),
         cost_estimate=pl.CostEstimate(
             flops=10 * count * width * ff,
@@ -716,32 +719,39 @@
         out_cotangent.reshape(count, width), starts + later, down_weight, split
     )
     gate_t, up_t = gate_weight.T, up_weight.T
-    norm_first, norm_last, _, _, (hidden_first, hidden_last) = plane_gather(
-        normed2, beside=(hidden_first, hidden_last)
-    )
-    sums_first, kept_first = feed_forward(
-        norm_first, hidden_first, gate_t, up_t, down_weight, 6
+    quarter = count // 4
+    norm_first, norm_last, _, _, ((near_hidden, hidden_last), own_results) = plane_gather(
+        normed2,
+        beside=(hidden_first, hidden_last),
+        own=lambda norms: feed_forward(norms, hidden_first, 0, gate_t, up_t, down_weight, 2),
+    )
+    sums_own, kept_own = own_results
+    sums_near, kept_near = feed_forward(
+        norm_first[2:], near_hidden, quarter, gate_t, up_t, down_weight, 4
     )
     piece = norm_last[0].shape[0]
     norm_last = assemble(
         norm_last, (((0, 0, piece), (1, 0, piece)), ((2, 0, piece), (3, 0, piece)))
     )
-    norm_last, sums_first = tied((norm_last, sums_first))
-    sums_last, kept_last = feed_forward(norm_last, hidden_last, gate_t, up_t, down_weight, 4)
+    norm_last, sums_near = tied((norm_last, sums_near))
+    sums_last, kept_last = feed_forward(norm_last, hidden_last, 0, gate_t, up_t, down_weight, 4)
     moved = scatter_far(sums_last, ("y", "x"))
-    moved, kept_first, kept_last, norm_first, norm_last = tied(
-        (moved, kept_first, kept_last, norm_first, norm_last)
+    moved, kept_own, kept_near, kept_last, norm_first, norm_last = tied(
+        (moved, kept_own, kept_near, kept_last, norm_first, norm_last)
     )
     rows = norm_last[0].shape[0]
-    norm_first, norm_last = assemble(
+    norm_parts = assemble(
         tuple(norm_first) + tuple(norm_last),
-        (tuple((i, 0, rows) for i in range(6)), ((6, 0, rows), (7, 0, rows))),
-    )
+        tuple(tuple((i, 0, rows) for i in group) for group in ((0, 1), (2, 3, 4, 5), (6, 7))),
+    )
+    low_parts = (grad_low[0][:quarter], grad_low[0][quarter:], grad_low[1])
     ffn_grads = []
     for k in range(3):
-        right_first = norm_first if k < 2 else grad_low[0]
-        right_last = norm_last if k < 2 else grad_low[1]
-        part = dot(kept_first[k], right_first, 0, 0) + dot(kept_last[k], right_last, 0, 0)
+        rights = norm_parts if k < 2 else low_parts
+        part = sum(
+            dot(kept[k], right, 0, 0)
+            for kept, right in zip((kept_own, kept_near, kept_last), rights)
+        )
         ffn_grads.append(part.astype(bf16))
     ffn_grads = jnp.concatenate(ffn_grads + [jnp.zeros((32, width), bf16)], axis=0)
     ffn_grads = lax.psum_scatter(ffn_grads, SEQ, scatter_dimension=0, tiled=True)
@@ -754,11 +764,11 @@
     rows_two = lax.dynamic_slice_in_dim(two_back.reshape(count, 1), place * own, own, axis=0)
     rows_n1 = jnp.concatenate([edge_n1, rows_n1], axis=0)
 
-    moved = scatter_near([sums_first[i] for i in (1, 2, 4, 5)], moved, ("y", "x"))
+    moved = scatter_near(list(sums_near), moved, ("y", "x"))
     gates, lags, conv = mixer_gates(rows_n1, in_all, taps, rows_one, rows_two)
     moved, gates, lags, conv = tied((moved, gates, lags, conv))
-    top = ring_sums(sums_first[0], *moved[:2])
-    bottom = ring_sums(sums_first[3], *moved[2:])
+    top = ring_sums(sums_own[0], *moved[:2])
+    bottom = ring_sums(sums_own[1], *moved[2:])
     moved = tuple(turn(top[k], "x", k) for k in (1, 2, 3))
     moved = moved + tuple(turn(bottom[k], "y", k) for k in (1, 2, 3))
     moved, ffn_grads = tied((moved, ffn_grads))

time: 339 us -> 336 us (level)
  waiting for transfers between devices: 93 us -> 87.6 us
    ppermute x42, waiting for transfers between devices: 76.2 us -> 70.5 us  [turn(): lax.ppermute(value, axis, [(i, (i + steps) % RING) for i in range(RING)])]
    dot_general x11 -> x14, matrix products: 12.2 us -> 12.8 us  [dot(): lax.dot_general(left, right, (((left_dim,), (right_dim,)), ((), ())), pre...]
    pallas_call x2 -> x3, Pallas kernels: 13.9 us -> 14.4 us  [feed_forward(): pl.pallas_call(body, in_specs=in_vmem(len(norms)) + [pl.BlockSpec(memory_...]
  transfers between devices with their start and end apart: 56 -> 56, of which waited for: 21 -> 19; matrix products, arithmetic and copies ran while one was open for 14% -> 15% of each run, Pallas kernels for 14% -> 15%
where the time goes in v1:
time: 336 us; the launch traced here: 331 us
  starting transfers between devices  101 us (30%)
  waiting for transfers between devices  87.6 us (26%)
  Pallas kernels  53.9 us (16%)
  local copies, waits for them, and re-layouts  36.2 us (11%)
  other arithmetic  21.8 us (6%)
  between operations  17.7 us (5%)
  matrix products  12.8 us (4%)
    ppermute x42, waiting for transfers between devices, turn(): lax.ppermute(value, axis, [(i, (i + steps) % RING) for i in range(RING)])  70.5 us
    ppermute x42, starting transfers between devices, turn(): lax.ppermute(value, axis, [(i, (i + steps) % RING) for i in range(RING)])  55.8 us
    unnamed x89, local copies, waits for them, and re-layouts  20.2 us
    pallas_call x3, Pallas kernels, feed_forward(): pl.pallas_call(body, in_specs=in_vmem(len(norms)) + [pl.BlockSpec(memory_...  14.4 us
    dot_general x14, matrix products, dot(): lax.dot_general(left, right, (((left_dim,), (right_dim,)), ((), ())), pre...  12.8 us
    ppermute x4, starting transfers between devices, swap_cores(): return lax.ppermute(value, 'core', [(0, 1), (1, 0)])  12.6 us
    pallas_call x1, Pallas kernels, relative_rows(): pl.pallas_call(body, grid_spec=pltpu.PrefetchScalarGridSpec(num_scalar_pr...  7.95 us
    all_to_all x1, starting transfers between devices, exchange(): exchanged = lax.all_to_all(exchanged, TP, 0, 0, tiled=True)  7.79 us
  transfers between devices with their start and end apart: 56, of which 19 were waited for; matrix products, arithmetic and copies ran while one was open for 15% of the time, Pallas kernels for 15%

profile of v1, /device:TPU:65, one launch (start us, length us, event | category | flops | bytes accessed | tf_op | source)
XLA Modules:
  0.0 330.6 jit_solution(4999914678822911608)
XLA Ops:
  11.6 6.8 %all-to-all-start = ((bf16[16,32,1024]{2,1,0:T(8,128)(2,1)}), bf16[16,32,1024]{2,1,0:T(8,128)(2,1)}, u32[]{:S(2)}, u32[]{:S(2)}) async-start(bf16[16,32,1024]{2,1,0:T(8,128)(2,1)} %broadcast_in_dim.10), calls=%async_computation | async-start | bytes 2097152 | tf_op jit(solution)/shard_map/all_to_all | solution.py:664
  18.4 3.4 %copy-done.3 = f32[2,1024,1024]{2,1,0:T(8,128)S(1)} copy-done((f32[2,1024,1024]{2,1,0:T(8,128)S(1)}, f32[2,1024,1024]{2,1,0:T(8,128)}, u32[]{:S(2)}) %copy-start.3) | copy-done | bytes 8388632
  21.8 4.6 %norm_and_project.1 = (bf16[2048,1024]{1,0:T(8,128)(2,1)}, f32[192,2048]{1,0:T(8,128)S(1)}) custom-call(f32[2048,1024]{1,0:T(8,128)S(1)} %bitcast.170, f32[1,1024]{1,0:T(1,128)S(1)} %bitcast.176, bf16[192,1024]{1,0:T(8,128)(2,1)S(1)} %bitcast.173), custom_call_target="tpu_custom_call" | custom-call | flops 805306368 | bytes 12582912 | tf_op jit(solution)/shard_map/norm_and_project/pallas_call | solution.py:383
  27.1 4.1 %collective-permute-start = (bf16[2,8,1024]{2,1,0:T(8,128)(2,1)S(1)}, bf16[2,8,1024]{2,1,0:T(8,128)(2,1)S(1)}, u32[]{:S(2)}, u32[]{:S(2)}) collective-permute-start(bf16[2,8,1024]{2,1,0:T(8,128)(2,1)S(1)} %slice.274), channel_id=1, source_target_pairs={{0,16},{1,17},{2,18},{3,19},{4,20},{5,21},{6,22},{7,23},{8,24},{9,... | collective-permute-start | bytes 98312 | tf_op jit(solution)/shard_map/ppermute | solution.py:690
  33.2 1.6 all-to-all-done
  34.7 2.5 collective-permute-start.1
  38.6 3.7 %all-to-all-start.1 = ((bf16[16,64,128]{2,1,0:T(8,128)(2,1)}), bf16[16,64,128]{2,1,0:T(8,128)(2,1)S(1)}, u32[]{:S(2)}, u32[]{:S(2)}) async-start(bf16[16,64,128]{2,1,0:T(8,128)(2,1)} %pad_maximum_fusion.4), calls=%async_computation.1 | async-start | bytes 524288 | tf_op jit(solution)/shard_map/all_to_all | solution.py:708
  42.3 1.7 select_bitcast_fusion.2
  44.3 6.5 %all-to-all-done.1 = bf16[16,64,128]{2,1,0:T(8,128)(2,1)S(1)} async-done(((bf16[16,64,128]{2,1,0:T(8,128)(2,1)}), bf16[16,64,128]{2,1,0:T(8,128)(2,1)S(1)}, u32[]{:S(2)}, u32[]{:S(2)}) %all-to-all-start.1) | async-done | bytes 262176 | tf_op jit(solution)/shard_map/all_to_all | solution.py:708
  51.5 1.6 multiply_reduce_fusion
  53.7 1.8 collective-permute-start.3
  57.0 1.7 collective-permute-done.2.refs_2_
  58.6 1.7 collective-permute-done.3.refs_3_
  60.4 4.2 %collective-permute-done.4.refs_4_ = bf16[64,1024]{1,0:T(8,128)(2,1)S(1)} collective-permute-done((bf16[64,1024]{1,0:T(8,128)(2,1)S(1)}, bf16[64,1024]{1,0:T(8,128)(2,1)S(1)}, u32[]{:S(2)}, u32[]{:S(2)}) %collective-permute-start.4) | collective-permute-done | bytes 131104 | tf_op jit(solution)/shard_map/ppermute | solution.py:20
  68.4 1.7 collective-permute-start.9
  71.4 3.4 %copy-done.4 = f32[2,1024,1024]{2,1,0:T(8,128)S(1)} copy-done((f32[2,1024,1024]{2,1,0:T(8,128)S(1)}, f32[2,1024,1024]{2,1,0:T(8,128)}, u32[]{:S(2)}) %copy-start.4) | copy-done | bytes 8388632
  74.8 7.9 %relative_rows.1 = (bf16[1536,1024]{1,0:T(8,128)(2,1)S(1)}, bf16[512,1024]{1,0:T(8,128)(2,1)S(1)}, f32[1536,288]{1,0:T(8,128)S(1)}, f32[512,288]{1,0:T(8,128)S(1)}) custom-call(s32[32]{0:T(128)S(1)} %get-tuple-element.327.table, f32[2048,1024]{1,0:T(8,128)S(1)} %bitcast.172, bf16[288,1024]{1,0:T(8,128)(2,1)S(1)} %copy-done.19), custom_call_target="tpu_custom_call" | custom-call | flops 1207959552 | bytes 12582912 | tf_op jit(solution)/shard_map/relative_rows/pallas_call | solution.py:294
  82.8 3.3 %feed_forward.3 = (bf16[256,2048]{1,0:T(8,128)(2,1)S(1)}, bf16[256,2048]{1,0:T(8,128)(2,1)S(1)}, bf16[512,288]{1,0:T(8,128)(2,1)S(1)}, bf16[512,288]{1,0:T(8,128)(2,1)S(1)}, bf16[512,288]{1,0:T(8,128)(2,1)S(1)}) custom-call(bf16[256,1024]{1,0:T(8,128)(2,1)S(1)} %get-tuple-element.256.refs_0_, bf16[256,1024]{1,0:T(8,128)(2,1)S(1)} %get-tuple-element.257.refs_1_, ...), custom_call_target="tpu_custom_call" | custom-call | flops 1509949440 | bytes 3145728 | tf_op jit(solution)/shard_map/feed_forward/pallas_call | solution.py:599
  88.1 3.8 %collective-permute-done.9.refs_1_.refs_3_ = bf16[256,1024]{1,0:T(8,128)(2,1)S(1)} collective-permute-done((bf16[256,1024]{1,0:T(8,128)(2,1)S(1)}, bf16[256,1024]{1,0:T(8,128)(2,1)S(1)}, u32[]{:S(2)}, u32[]{:S(2)}) %collective-permute-start.9) | collective-permute-done | bytes 524320 | tf_op jit(solution)/shard_map/ppermute | solution.py:20
  92.0 1.7 collective-permute-start.12
  94.7 2.9 collective-permute-start.15
  97.6 7.8 %feed_forward.4 = (bf16[256,2048]{1,0:T(8,128)(2,1)}, bf16[256,2048]{1,0:T(8,128)(2,1)}, bf16[256,2048]{1,0:T(8,128)(2,1)}, bf16[256,2048]{1,0:T(8,128)(2,1)}, b...) custom-call(bf16[256,1024]{1,0:T(8,128)(2,1)S(1)} %collective-permute-done.8.refs_0_.refs_, ...), custom_call_target="tpu_custom_call" | custom-call | flops 3019898880 | bytes 6291456 | tf_op jit(solution)/shard_map/feed_forward/pallas_call | solution.py:599
  105.6 3.3 %feed_forward.5 = (bf16[128,2048]{1,0:T(8,128)(2,1)S(1)}, bf16[128,2048]{1,0:T(8,128)(2,1)S(1)}, bf16[128,2048]{1,0:T(8,128)(2,1)S(1)}, bf16[128,2048]{1,0:T(8,1...) custom-call(bf16[256,1024]{1,0:T(8,128)(2,1)S(1)} %get-tuple-element.262.refs, ...), custom_call_target="tpu_custom_call" | custom-call | flops 1509949440 | bytes 3145728 | tf_op jit(solution)/shard_map/feed_forward/pallas_call | solution.py:599
  109.3 2.3 collective-permute-start.17
  111.7 2.9 collective-permute-start.19
  114.6 4.3 %collective-permute-done.16.refs_4_ = bf16[128,2048]{1,0:T(8,128)(2,1)S(1)} collective-permute-done((bf16[128,2048]{1,0:T(8,128)(2,1)S(1)}, bf16[128,2048]{1,0:T(8,128)(2,1)S(1)}, u32[]{:S(2)}, u32[]{:S(2)}) %collective-permute-start.16) | collective-permute-done | bytes 524320 | tf_op jit(solution)/shard_map/ppermute | solution.py:20
  118.9 2.3 collective-permute-done.18.refs_6_
  127.1 1.6 maximum_maximum_fusion
  128.8 2.6 add_halves.1
  131.5 2.7 collective-permute-start.21
  134.2 2.8 collective-permute-start.23
  139.6 3.5 %slice.293 = bf16[8,16,3,8,1024]{4,3,2,1,0:T(8,128)(2,1)S(1)} slice(bf16[8,16,4,8,1024]{4,3,2,1,0:T(8,128)(2,1)} %bitcast.189), slice={[0:8], [0:16], [0:3], [0:8], [0:1024]} | slice | bytes 12582912 | tf_op jit(solution)/shard_map/slice | solution.py:679
  144.1 3.4 %copy.80 = bf16[8,16,3,8,1024]{4,3,0,1,2:T(8,128)(2,1)} copy(bf16[8,16,3,8,1024]{4,3,2,1,0:T(8,128)(2,1)S(1)} %slice.293) | data formatting | bytes 12582912
  147.8 2.9 copy-done.2
  150.6 2.4 mixer_gates.1
  153.8 2.6 ring_sums.3
  158.4 1.9 collective-permute-start.29
  160.3 2.6 ring_sums.2
  163.9 3.1 collective-permute-start.25
  169.0 1.9 constant_dynamic-slice_fusion.refs_11_
  172.2 1.7 collective-permute-done.25.refs_3_
  174.1 5.0 %residual_back.1 = (bf16[128,1024]{1,0:T(8,128)(2,1)}, f32[128,1024]{1,0:T(8,128)}, bf16[128,1024]{1,0:T(8,128)(2,1)}, f32[1,1024]{1,0:T(1,128)}, f32[128,1024]{1,0:T(8,128)}, /*index=5*/f32[16,1024]{1,0:T(8,128)}) custom-call(f32[64,2048]{1,0:T(8,128)} %copy-done.21, f32[64,2048]{1,0:T(8,128)} %copy-done.20, ...), custom_call_target="tpu_custom_call" | custom-call | flops 268435456 | bytes 7448064 | tf_op jit(solution)/shard_map/residual_back/pallas_call | solution.py:192
  179.1 1.9 convolution_convert_fusion
  181.2 9.0 %collective-permute-start.31 = (bf16[16,32,1024]{2,1,0:T(8,128)(2,1)S(1)}, bf16[16,32,1024]{2,1,0:T(8,128)(2,1)S(1)}, u32[]{:S(2)}, u32[]{:S(2)}) collective-permute-start(bf16[16,32,1024]{2,1,0:T(8,128)(2,1)S(1)} %select_bitcast_fusion), channel_id=1, source_target_pairs={{0,16},{16,0},{1,17},{17,1},{2,18},{18,2},{3,19},{19,3},{4,20},{20... | collective-permute-start | bytes 3145736 | tf_op jit(solution)/shard_map/ppermute | solution.py:239
  190.2 5.3 %collective-permute-start.30 = (f32[16,1024]{1,0:T(8,128)S(1)}, f32[16,1024]{1,0:T(8,128)S(1)}, u32[]{:S(2)}, u32[]{:S(2)}) collective-permute-start(f32[16,1024]{1,0:T(8,128)S(1)} %copy-done.39), channel_id=1, source_target_pairs={{1,0},{2,1},{3,2},{4,3},{5,4},{6,5},{7,6},{9,8},{10,9},{11,10},{12... | collective-permute-start | bytes 196616 | tf_op jit(solution)/shard_map/ppermute | solution.py:799
  197.4 1.7 mixer_back.1
  200.6 3.2 collective-permute-start.32
  204.6 2.6 collective-permute-start.35
  207.9 5.5 %collective-permute-start.37 = (bf16[64,1024]{1,0:T(8,128)(2,1)S(1)}, bf16[64,1024]{1,0:T(8,128)(2,1)S(1)}, u32[]{:S(2)}, u32[]{:S(2)}) collective-permute-start(bf16[64,1024]{1,0:T(8,128)(2,1)S(1)} %get-tuple-element.293.refs_1_), channel_id=1, source_target_pairs={{0,4},{4,8},{8,12},{12,0},{1,5},{5,9},{9,13},{13,1},{2,6},{6,10},{... | collective-permute-start | bytes 393224 | tf_op jit(solution)/shard_map/ppermute | solution.py:20
  213.4 1.5 collective-permute-done.34.refs_4_
  215.0 1.6 collective-permute-done.37.refs_7_
  216.6 7.8 %all-to-all-start.2 = ((bf16[16,472,128]{2,1,0:T(8,128)(2,1)}), bf16[16,472,128]{2,1,0:T(8,128)(2,1)}, u32[]{:S(2)}, u32[]{:S(2)}) async-start(bf16[16,472,128]{2,1,0:T(8,128)(2,1)} %copy-done.6), calls=%async_computation.3 | async-start | bytes 3866624 | tf_op jit(solution)/shard_map/all_to_all | solution.py:823
  226.4 2.6 collective-permute-start.38
  229.1 2.4 collective-permute-start.40
  231.5 43.7 %collective-permute-done.38.refs_0_.refs_2_ = bf16[256,1024]{1,0:T(8,128)(2,1)S(1)} collective-permute-done((bf16[256,1024]{1,0:T(8,128)(2,1)S(1)}, bf16[256,1024]{1,0:T(8,128)(2,1)S(1)}, u32[]{:S(2)}, u32[]{:S(2)}) %collective-permute-start.38) | collective-permute-done | bytes 524320 | tf_op jit(solution)/shard_map/ppermute | solution.py:20
  275.1 2.3 collective-permute-done.40.refs_2_.refs_4_
  278.9 3.4 %convolution_convert_fusion.1 = bf16[192,1024]{1,0:T(8,128)(2,1)S(1)} fusion(bf16[2048,1024]{1,0:T(8,128)(2,1)} %get-tuple-element.168, bf16[16,472,128]{2,1,0:T(8,128)(2,1)} %all-to-all-done.2), kind=kOutput, calls=%fused_computation.16 | convolution fusion | flops 805502976 | bytes 5373952 | tf_op jit(solution)/shard_map/dot_general | solution.py:618
  285.5 4.3 %all-to-all-start.3 = ((bf16[4,136,1024]{2,1,0:T(8,128)(2,1)}), bf16[4,136,1024]{2,1,0:T(8,128)(2,1)}, u32[]{:S(2)}, u32[]{:S(2)}) async-start(bf16[4,136,1024]{2,1,0:T(8,128)(2,1)} %broadcast_in_dim.14), calls=%async_computation.4 | async-start | bytes 2228224 | tf_op jit(solution)/shard_map/all_to_all | solution.py:842
  291.3 2.4 collective-permute-start.43
  294.5 3.1 collective-permute-start.45
  297.5 6.7 %convert.33 = f32[2,1024,1024]{2,1,0:T(8,128)} convert(bf16[2,1024,1024]{2,1,0:T(8,128)(2,1)} %bitcast.191) | non-fusion elementwise | flops 2097152 | bytes 12582912 | tf_op jit(solution)/shard_map/reshape | solution.py:864
  304.2 6.3 %all-gather.7.cloned.1.call-done = bf16[896,1024]{1,0:T(8,128)(2,1)} async-done(((bf16[112,1024]{1,0:T(8,128)(2,1)}), bf16[896,1024]{1,0:T(8,128)(2,1)}) %all-gather.7.cloned.1.call-update) | async-done | bytes 1835024 | tf_op jit(solution)/shard_map/all_gather | solution.py:824
  310.5 5.1 %absolute_rows.1 = f32[2048,1024]{1,0:T(8,128)} custom-call(s32[32]{0:T(128)S(1)} %get-tuple-element.328.table, bf16[256,1024]{1,0:T(8,128)(2,1)S(1)} %get-tuple-element.302.refs_0_, bf16[256,1024]{1,0:T(8,128)(2,1)S(1)} %get-tuple-element.303.refs_1_, bf16[256,1024]{1,0:T(8,128)(2,1)S(1)} %collective-permute-done.38.refs_0_.refs_2_, ...), custom_call_target="tpu_custom_call" | custom-call | flops 2097152 | bytes 12582912 | tf_op jit(solution)/shard_map/absolute_rows/pallas_call | solution.py:350
  315.6 1.9 slice_convert_fusion
  (255 shorter events, 54.5 us)
Async XLA Ops:
  8.0 131.6 %all-gather.9.cloned.1.call-start = ((), (), s32[]{:S(2)}) async-start(), calls=%async_computation.8 | async-start | bytes 8454144 | tf_op jit(solution)/shard_map/all_gather | solution.py:674
  11.6 23.2 %all-to-all-start = ((bf16[16,32,1024]{2,1,0:T(8,128)(2,1)}), bf16[16,32,1024]{2,1,0:T(8,128)(2,1)}, u32[]{:S(2)}, u32[]{:S(2)}) async-start(bf16[16,32,1024]{2,1,0:T(8,128)(2,1)} %broadcast_in_dim.10), calls=%async_computation | async-start | bytes 2097152 | tf_op jit(solution)/shard_map/all_to_all | solution.py:664
  27.1 5.5 %collective-permute-start = (bf16[2,8,1024]{2,1,0:T(8,128)(2,1)S(1)}, bf16[2,8,1024]{2,1,0:T(8,128)(2,1)S(1)}, u32[]{:S(2)}, u32[]{:S(2)}) collective-permute-start(bf16[2,8,1024]{2,1,0:T(8,128)(2,1)S(1)} %slice.274), channel_id=1, source_target_pairs={{0,16},{1,17},{2,18},{3,19},{4,20},{5,21},{6,22},{7,23},{8,24},{9,... | collective-permute-start | bytes 98312 | tf_op jit(solution)/shard_map/ppermute | solution.py:690
  34.7 7.6 %collective-permute-start.1 = (bf16[16,32,1024]{2,1,0:T(8,128)(2,1)}, bf16[16,32,1024]{2,1,0:T(8,128)(2,1)}, u32[]{:S(2)}, u32[]{:S(2)}) collective-permute-start(bf16[16,32,1024]{2,1,0:T(8,128)(2,1)} %all-to-all-done), channel_id=1, source_target_pairs={{0,16},{16,0},{1,17},{17,1},{2,18},{18,2},{3,19},{19,3},{4,20},{20... | collective-permute-start | bytes 3145736 | tf_op jit(solution)/shard_map/ppermute | solution.py:239
  38.6 12.2 %all-to-all-start.1 = ((bf16[16,64,128]{2,1,0:T(8,128)(2,1)}), bf16[16,64,128]{2,1,0:T(8,128)(2,1)S(1)}, u32[]{:S(2)}, u32[]{:S(2)}) async-start(bf16[16,64,128]{2,1,0:T(8,128)(2,1)} %pad_maximum_fusion.4), calls=%async_computation.1 | async-start | bytes 524288 | tf_op jit(solution)/shard_map/all_to_all | solution.py:708
  42.3 129.9 %reduce-scatter.2.cloned.1.call-start = ((), (), s32[]{:S(2)}) async-start(), calls=%async_computation.5 | async-start | bytes 2064384 | tf_op jit(solution)/shard_map/reduce_scatter | solution.py:757
  51.5 19.8 %copy-start.36 = (s32[32]{0:T(128)S(1)}, s32[32]{0:T(128)}, u32[]{:S(2)}) copy-start(s32[32]{0:T(128)} %constant.117.clone) | copy-start | bytes 388
  51.5 19.8 %copy-start.37 = (s32[32]{0:T(128)S(1)}, s32[32]{0:T(128)}, u32[]{:S(2)}) copy-start(s32[32]{0:T(128)} %constant.125) | copy-start | bytes 388
  51.5 19.8 %copy-start.38 = (s32[32]{0:T(128)S(1)}, s32[32]{0:T(128)}, u32[]{:S(2)}) copy-start(s32[32]{0:T(128)} %constant.126) | copy-start | bytes 388
  51.5 19.8 %copy-start.19 = (bf16[288,1024]{1,0:T(8,128)(2,1)S(1)}, bf16[288,1024]{1,0:T(8,128)(2,1)}, u32[]{:S(2)}) copy-start(bf16[288,1024]{1,0:T(8,128)(2,1)} %refs_5_.3) | copy-start | bytes 1769476
  53.1 29.7 %copy-start.29 = (f32[128,1024]{1,0:T(8,128)}, f32[128,1024]{1,0:T(8,128)S(1)}, u32[]{:S(2)}) copy-start(f32[128,1024]{1,0:T(8,128)S(1)} %get-tuple-element.363.refs_8_) | copy-start | bytes 1572868
  53.6 5.0 %collective-permute-start.2 = (bf16[64,1024]{1,0:T(8,128)(2,1)S(1)}, bf16[64,1024]{1,0:T(8,128)(2,1)S(1)}, u32[]{:S(2)}, u32[]{:S(2)}) collective-permute-start(bf16[64,1024]{1,0:T(8,128)(2,1)S(1)} %get-tuple-element.170.refs_0_), channel_id=1, source_target_pairs={{0,3},{1,0},{2,1},{3,2},{4,7},{5,4},{6,5},{7,6},{8,11},{9,8},{10,9... | collective-permute-start | bytes 393224 | tf_op jit(solution)/shard_map/ppermute | solution.py:20
  53.7 6.7 %collective-permute-start.3 = (bf16[64,1024]{1,0:T(8,128)(2,1)S(1)}, bf16[64,1024]{1,0:T(8,128)(2,1)S(1)}, u32[]{:S(2)}, u32[]{:S(2)}) collective-permute-start(bf16[64,1024]{1,0:T(8,128)(2,1)S(1)} %get-tuple-element.170.refs_0_), channel_id=1, source_target_pairs={{0,2},{1,3},{2,0},{3,1},{4,6},{5,7},{6,4},{7,5},{8,10},{9,11},{10,... | collective-permute-start | bytes 393224 | tf_op jit(solution)/shard_map/ppermute | solution.py:20
  55.5 9.1 %collective-permute-start.4 = (bf16[64,1024]{1,0:T(8,128)(2,1)S(1)}, bf16[64,1024]{1,0:T(8,128)(2,1)S(1)}, u32[]{:S(2)}, u32[]{:S(2)}) collective-permute-start(bf16[64,1024]{1,0:T(8,128)(2,1)S(1)} %get-tuple-element.170.refs_0_), channel_id=1, source_target_pairs={{0,1},{1,2},{2,3},{3,0},{4,5},{5,6},{6,7},{7,4},{8,9},{9,10},{10,1... | collective-permute-start | bytes 393224 | tf_op jit(solution)/shard_map/ppermute | solution.py:20
  55.5 9.1 %collective-permute-start.5 = (bf16[64,1024]{1,0:T(8,128)(2,1)S(1)}, bf16[64,1024]{1,0:T(8,128)(2,1)S(1)}, u32[]{:S(2)}, u32[]{:S(2)}) collective-permute-start(bf16[64,1024]{1,0:T(8,128)(2,1)S(1)} %get-tuple-element.171.refs_1_), channel_id=1, source_target_pairs={{0,12},{4,0},{8,4},{12,8},{1,13},{5,1},{9,5},{13,9},{2,14},{6,2},{... | collective-permute-start | bytes 393224 | tf_op jit(solution)/shard_map/ppermute | solution.py:20
  56.1 8.5 %collective-permute-start.6 = (bf16[64,1024]{1,0:T(8,128)(2,1)S(1)}, bf16[64,1024]{1,0:T(8,128)(2,1)S(1)}, u32[]{:S(2)}, u32[]{:S(2)}) collective-permute-start(bf16[64,1024]{1,0:T(8,128)(2,1)S(1)} %get-tuple-element.171.refs_1_), channel_id=1, source_target_pairs={{0,8},{4,12},{8,0},{12,4},{1,9},{5,13},{9,1},{13,5},{2,10},{6,14},... | collective-permute-start | bytes 393224 | tf_op jit(solution)/shard_map/ppermute | solution.py:20
  58.6 6.6 %collective-permute-start.7 = (bf16[64,1024]{1,0:T(8,128)(2,1)S(1)}, bf16[64,1024]{1,0:T(8,128)(2,1)S(1)}, u32[]{:S(2)}, u32[]{:S(2)}) collective-permute-start(bf16[64,1024]{1,0:T(8,128)(2,1)S(1)} %get-tuple-element.171.refs_1_), channel_id=1, source_target_pairs={{0,4},{4,8},{8,12},{12,0},{1,5},{5,9},{9,13},{13,1},{2,6},{6,10},{... | collective-permute-start | bytes 393224 | tf_op jit(solution)/shard_map/ppermute | solution.py:20
  66.6 21.5 %collective-permute-start.10 = (bf16[256,1024]{1,0:T(8,128)(2,1)S(1)}, bf16[256,1024]{1,0:T(8,128)(2,1)S(1)}, u32[]{:S(2)}, u32[]{:S(2)}) collective-permute-start(bf16[256,1024]{1,0:T(8,128)(2,1)S(1)} %get-tuple-element.257.refs_1_), channel_id=1, source_target_pairs={{0,3},{1,0},{2,1},{3,2},{4,7},{5,4},{6,5},{7,6},{8,11},{9,8},{10,9... | collective-permute-start | bytes 1572872 | tf_op jit(solution)/shard_map/ppermute | solution.py:20
  67.8 20.3 %collective-permute-start.11 = (bf16[256,1024]{1,0:T(8,128)(2,1)S(1)}, bf16[256,1024]{1,0:T(8,128)(2,1)S(1)}, u32[]{:S(2)}, u32[]{:S(2)}) collective-permute-start(bf16[256,1024]{1,0:T(8,128)(2,1)S(1)} %get-tuple-element.257.refs_1_), channel_id=1, source_target_pairs={{0,1},{1,2},{2,3},{3,0},{4,5},{5,6},{6,7},{7,4},{8,9},{9,10},{10,1... | collective-permute-start | bytes 1572872 | tf_op jit(solution)/shard_map/ppermute | solution.py:20
  68.1 19.9 %collective-permute-start.8 = (bf16[256,1024]{1,0:T(8,128)(2,1)S(1)}, bf16[256,1024]{1,0:T(8,128)(2,1)S(1)}, u32[]{:S(2)}, u32[]{:S(2)}) collective-permute-start(bf16[256,1024]{1,0:T(8,128)(2,1)S(1)} %get-tuple-element.256.refs_0_), channel_id=1, source_target_pairs={{0,12},{4,0},{8,4},{12,8},{1,13},{5,1},{9,5},{13,9},{2,14},{6,2},{... | collective-permute-start | bytes 1572872 | tf_op jit(solution)/shard_map/ppermute | solution.py:20
  68.4 23.4 %collective-permute-start.9 = (bf16[256,1024]{1,0:T(8,128)(2,1)S(1)}, bf16[256,1024]{1,0:T(8,128)(2,1)S(1)}, u32[]{:S(2)}, u32[]{:S(2)}) collective-permute-start(bf16[256,1024]{1,0:T(8,128)(2,1)S(1)} %get-tuple-element.256.refs_0_), channel_id=1, source_target_pairs={{0,4},{4,8},{8,12},{12,0},{1,5},{5,9},{9,13},{13,1},{2,6},{6,10},{... | collective-permute-start | bytes 1572872 | tf_op jit(solution)/shard_map/ppermute | solution.py:20
  92.0 13.4 %collective-permute-start.12 = (bf16[128,1024]{1,0:T(8,128)(2,1)S(1)}, bf16[128,1024]{1,0:T(8,128)(2,1)S(1)}, u32[]{:S(2)}, u32[]{:S(2)}) collective-permute-start(bf16[128,1024]{1,0:T(8,128)(2,1)S(1)} %get-tuple-element.192), channel_id=1, source_target_pairs={{0,4},{4,8},{8,12},{12,0},{1,5},{5,9},{9,13},{13,1},{2,6},{6,10},{... | collective-permute-start | bytes 786440 | tf_op jit(solution)/shard_map/ppermute | solution.py:20
  93.7 11.7 %collective-permute-start.13 = (bf16[128,1024]{1,0:T(8,128)(2,1)S(1)}, bf16[128,1024]{1,0:T(8,128)(2,1)S(1)}, u32[]{:S(2)}, u32[]{:S(2)}) collective-permute-start(bf16[128,1024]{1,0:T(8,128)(2,1)S(1)} %get-tuple-element.193), channel_id=1, source_target_pairs={{0,12},{4,0},{8,4},{12,8},{1,13},{5,1},{9,5},{13,9},{2,14},{6,2},{... | collective-permute-start | bytes 786440 | tf_op jit(solution)/shard_map/ppermute | solution.py:20
  94.7 10.7 %collective-permute-start.14 = (bf16[128,1024]{1,0:T(8,128)(2,1)S(1)}, bf16[128,1024]{1,0:T(8,128)(2,1)S(1)}, u32[]{:S(2)}, u32[]{:S(2)}) collective-permute-start(bf16[128,1024]{1,0:T(8,128)(2,1)S(1)} %get-tuple-element.194), channel_id=1, source_target_pairs={{0,1},{1,2},{2,3},{3,0},{4,5},{5,6},{6,7},{7,4},{8,9},{9,10},{10,1... | collective-permute-start | bytes 786440 | tf_op jit(solution)/shard_map/ppermute | solution.py:20
  94.7 10.7 %collective-permute-start.15 = (bf16[128,1024]{1,0:T(8,128)(2,1)S(1)}, bf16[128,1024]{1,0:T(8,128)(2,1)S(1)}, u32[]{:S(2)}, u32[]{:S(2)}) collective-permute-start(bf16[128,1024]{1,0:T(8,128)(2,1)S(1)} %get-tuple-element.195), channel_id=1, source_target_pairs={{0,3},{1,0},{2,1},{3,2},{4,7},{5,4},{6,5},{7,6},{8,11},{9,8},{10,9... | collective-permute-start | bytes 786440 | tf_op jit(solution)/shard_map/ppermute | solution.py:20
  108.9 10.0 %collective-permute-start.16 = (bf16[128,2048]{1,0:T(8,128)(2,1)S(1)}, bf16[128,2048]{1,0:T(8,128)(2,1)S(1)}, u32[]{:S(2)}, u32[]{:S(2)}) collective-permute-start(bf16[128,2048]{1,0:T(8,128)(2,1)S(1)} %get-tuple-element.214), channel_id=1, source_target_pairs={{0,4},{4,8},{8,12},{12,0},{1,5},{5,9},{9,13},{13,1},{2,6},{6,10},{... | collective-permute-start | bytes 1572872 | tf_op jit(solution)/shard_map/ppermute | solution.py:20
  109.3 9.6 %collective-permute-start.17 = (bf16[128,2048]{1,0:T(8,128)(2,1)S(1)}, bf16[128,2048]{1,0:T(8,128)(2,1)S(1)}, u32[]{:S(2)}, u32[]{:S(2)}) collective-permute-start(bf16[128,2048]{1,0:T(8,128)(2,1)S(1)} %get-tuple-element.215), channel_id=1, source_target_pairs={{0,12},{4,0},{8,4},{12,8},{1,13},{5,1},{9,5},{13,9},{2,14},{6,2},{... | collective-permute-start | bytes 1572872 | tf_op jit(solution)/shard_map/ppermute | solution.py:20
  111.7 9.5 %collective-permute-start.18 = (bf16[128,2048]{1,0:T(8,128)(2,1)S(1)}, bf16[128,2048]{1,0:T(8,128)(2,1)S(1)}, u32[]{:S(2)}, u32[]{:S(2)}) collective-permute-start(bf16[128,2048]{1,0:T(8,128)(2,1)S(1)} %get-tuple-element.216), channel_id=1, source_target_pairs={{0,1},{1,2},{2,3},{3,0},{4,5},{5,6},{6,7},{7,4},{8,9},{9,10},{10,1... | collective-permute-start | bytes 1572872 | tf_op jit(solution)/shard_map/ppermute | solution.py:20
  111.7 9.5 %collective-permute-start.19 = (bf16[128,2048]{1,0:T(8,128)(2,1)S(1)}, bf16[128,2048]{1,0:T(8,128)(2,1)S(1)}, u32[]{:S(2)}, u32[]{:S(2)}) collective-permute-start(bf16[128,2048]{1,0:T(8,128)(2,1)S(1)} %get-tuple-element.217), channel_id=1, source_target_pairs={{0,3},{1,0},{2,1},{3,2},{4,7},{5,4},{6,5},{7,6},{8,11},{9,8},{10,9... | collective-permute-start | bytes 1572872 | tf_op jit(solution)/shard_map/ppermute | solution.py:20
  128.8 148.7 %all-gather.5.cloned.1.call-start = ((), (), s32[]{:S(2)}) async-start(), calls=%async_computation.6 | async-start | bytes 4456448 | tf_op jit(solution)/shard_map/all_gather | solution.py:791
  131.4 21.7 %collective-permute-start.20 = (bf16[256,2048]{1,0:T(8,128)(2,1)}, bf16[256,2048]{1,0:T(8,128)(2,1)}, u32[]{:S(2)}, u32[]{:S(2)}) collective-permute-start(bf16[256,2048]{1,0:T(8,128)(2,1)} %get-tuple-element.235), channel_id=1, source_target_pairs={{0,4},{4,8},{8,12},{12,0},{1,5},{5,9},{9,13},{13,1},{2,6},{6,10},{... | collective-permute-start | bytes 3145736 | tf_op jit(solution)/shard_map/ppermute | solution.py:20
  131.5 21.6 %collective-permute-start.21 = (bf16[256,2048]{1,0:T(8,128)(2,1)}, bf16[256,2048]{1,0:T(8,128)(2,1)}, u32[]{:S(2)}, u32[]{:S(2)}) collective-permute-start(bf16[256,2048]{1,0:T(8,128)(2,1)} %get-tuple-element.236), channel_id=1, source_target_pairs={{0,12},{4,0},{8,4},{12,8},{1,13},{5,1},{9,5},{13,9},{2,14},{6,2},{... | collective-permute-start | bytes 3145736 | tf_op jit(solution)/shard_map/ppermute | solution.py:20
  134.1 19.7 %collective-permute-start.22 = (bf16[256,2048]{1,0:T(8,128)(2,1)}, bf16[256,2048]{1,0:T(8,128)(2,1)}, u32[]{:S(2)}, u32[]{:S(2)}) collective-permute-start(bf16[256,2048]{1,0:T(8,128)(2,1)} %get-tuple-element.237), channel_id=1, source_target_pairs={{0,1},{1,2},{2,3},{3,0},{4,5},{5,6},{6,7},{7,4},{8,9},{9,10},{10,1... | collective-permute-start | bytes 3145736 | tf_op jit(solution)/shard_map/ppermute | solution.py:20
  134.2 19.7 %collective-permute-start.23 = (bf16[256,2048]{1,0:T(8,128)(2,1)}, bf16[256,2048]{1,0:T(8,128)(2,1)}, u32[]{:S(2)}, u32[]{:S(2)}) collective-permute-start(bf16[256,2048]{1,0:T(8,128)(2,1)} %get-tuple-element.238), channel_id=1, source_target_pairs={{0,3},{1,0},{2,1},{3,2},{4,7},{5,4},{6,5},{7,6},{8,11},{9,8},{10,9... | collective-permute-start | bytes 3145736 | tf_op jit(solution)/shard_map/ppermute | solution.py:20
  153.0 18.5 %copy-start.7 = (f32[3,128,1024]{2,1,0:T(8,128)}, f32[3,128,1024]{2,1,0:T(8,128)S(1)}, u32[]{:S(2)}) copy-start(f32[3,128,1024]{2,1,0:T(8,128)S(1)} %get-tuple-element.283.refs_2_) | copy-start | bytes 4718596
  157.2 9.8 %collective-permute-start.27 = (bf16[64,2048]{1,0:T(8,128)(2,1)S(1)}, bf16[64,2048]{1,0:T(8,128)(2,1)S(1)}, u32[]{:S(2)}, u32[]{:S(2)}) collective-permute-start(bf16[64,2048]{1,0:T(8,128)(2,1)S(1)} %get-tuple-element.252), channel_id=1, source_target_pairs={{0,4},{4,8},{8,12},{12,0},{1,5},{5,9},{9,13},{13,1},{2,6},{6,10},{... | collective-permute-start | bytes 786440 | tf_op jit(solution)/shard_map/ppermute | solution.py:20
  157.2 14.9 %collective-permute-start.28 = (bf16[64,2048]{1,0:T(8,128)(2,1)S(1)}, bf16[64,2048]{1,0:T(8,128)(2,1)}, u32[]{:S(2)}, u32[]{:S(2)}) collective-permute-start(bf16[64,2048]{1,0:T(8,128)(2,1)S(1)} %get-tuple-element.253), channel_id=1, source_target_pairs={{0,8},{4,12},{8,0},{12,4},{1,9},{5,13},{9,1},{13,5},{2,10},{6,14},... | collective-permute-start | bytes 786440 | tf_op jit(solution)/shard_map/ppermute | solution.py:20
  158.4 13.8 %collective-permute-start.29 = (bf16[64,2048]{1,0:T(8,128)(2,1)S(1)}, bf16[64,2048]{1,0:T(8,128)(2,1)}, u32[]{:S(2)}, u32[]{:S(2)}) collective-permute-start(bf16[64,2048]{1,0:T(8,128)(2,1)S(1)} %get-tuple-element.254), channel_id=1, source_target_pairs={{0,12},{4,0},{8,4},{12,8},{1,13},{5,1},{9,5},{13,9},{2,14},{6,2},{... | collective-permute-start | bytes 786440 | tf_op jit(solution)/shard_map/ppermute | solution.py:20
  163.7 8.5 %collective-permute-start.24 = (bf16[64,2048]{1,0:T(8,128)(2,1)}, bf16[64,2048]{1,0:T(8,128)(2,1)}, u32[]{:S(2)}, u32[]{:S(2)}) collective-permute-start(bf16[64,2048]{1,0:T(8,128)(2,1)} %get-tuple-element.249), channel_id=1, source_target_pairs={{0,1},{1,2},{2,3},{3,0},{4,5},{5,6},{6,7},{7,4},{8,9},{9,10},{10,1... | collective-permute-start | bytes 786440 | tf_op jit(solution)/shard_map/ppermute | solution.py:20
  163.9 10.0 %collective-permute-start.25 = (bf16[64,2048]{1,0:T(8,128)(2,1)}, bf16[64,2048]{1,0:T(8,128)(2,1)}, u32[]{:S(2)}, u32[]{:S(2)}) collective-permute-start(bf16[64,2048]{1,0:T(8,128)(2,1)} %get-tuple-element.250), channel_id=1, source_target_pairs={{0,2},{1,3},{2,0},{3,1},{4,6},{5,7},{6,4},{7,5},{8,10},{9,11},{10,... | collective-permute-start | bytes 786440 | tf_op jit(solution)/shard_map/ppermute | solution.py:20
  167.8 6.3 %collective-permute-start.26 = (bf16[64,2048]{1,0:T(8,128)(2,1)}, bf16[64,2048]{1,0:T(8,128)(2,1)}, u32[]{:S(2)}, u32[]{:S(2)}) collective-permute-start(bf16[64,2048]{1,0:T(8,128)(2,1)} %get-tuple-element.251), channel_id=1, source_target_pairs={{0,3},{1,0},{2,1},{3,2},{4,7},{5,4},{6,5},{7,6},{8,11},{9,8},{10,9... | collective-permute-start | bytes 786440 | tf_op jit(solution)/shard_map/ppermute | solution.py:20
  174.1 23.2 %slice-start = ((s8[6291456]{0:T(1024)(128)(4,1)}), s8[2097152]{0:T(1024)(128)(4,1)S(1)}, s32[]{:S(2)}) async-start(s8[6291456]{0:T(1024)(128)(4,1)} %bitcast.166), calls=%async_computation.9 | async-start | bytes 4194304
  179.1 18.2 %slice-start.1 = ((s8[6291456]{0:T(1024)(128)(4,1)}), s8[4194304]{0:T(1024)(128)(4,1)S(1)}, s32[]{:S(2)}) async-start(s8[6291456]{0:T(1024)(128)(4,1)} %bitcast.166), calls=%async_computation.10 | async-start | bytes 8388608
  181.2 14.4 %collective-permute-start.31 = (bf16[16,32,1024]{2,1,0:T(8,128)(2,1)S(1)}, bf16[16,32,1024]{2,1,0:T(8,128)(2,1)S(1)}, u32[]{:S(2)}, u32[]{:S(2)}) collective-permute-start(bf16[16,32,1024]{2,1,0:T(8,128)(2,1)S(1)} %select_bitcast_fusion), channel_id=1, source_target_pairs={{0,16},{16,0},{1,17},{17,1},{2,18},{18,2},{3,19},{19,3},{4,20},{20... | collective-permute-start | bytes 3145736 | tf_op jit(solution)/shard_map/ppermute | solution.py:239
  190.2 7.1 %collective-permute-start.30 = (f32[16,1024]{1,0:T(8,128)S(1)}, f32[16,1024]{1,0:T(8,128)S(1)}, u32[]{:S(2)}, u32[]{:S(2)}) collective-permute-start(f32[16,1024]{1,0:T(8,128)S(1)} %copy-done.39), channel_id=1, source_target_pairs={{1,0},{2,1},{3,2},{4,3},{5,4},{6,5},{7,6},{9,8},{10,9},{11,10},{12... | collective-permute-start | bytes 196616 | tf_op jit(solution)/shard_map/ppermute | solution.py:799
  200.6 7.3 %collective-permute-start.32 = (bf16[64,1024]{1,0:T(8,128)(2,1)S(1)}, bf16[64,1024]{1,0:T(8,128)(2,1)S(1)}, u32[]{:S(2)}, u32[]{:S(2)}) collective-permute-start(bf16[64,1024]{1,0:T(8,128)(2,1)S(1)} %get-tuple-element.292.refs_0_), channel_id=1, source_target_pairs={{0,3},{1,0},{2,1},{3,2},{4,7},{5,4},{6,5},{7,6},{8,11},{9,8},{10,9... | collective-permute-start | bytes 393224 | tf_op jit(solution)/shard_map/ppermute | solution.py:20
  203.9 9.5 %collective-permute-start.33 = (bf16[64,1024]{1,0:T(8,128)(2,1)S(1)}, bf16[64,1024]{1,0:T(8,128)(2,1)S(1)}, u32[]{:S(2)}, u32[]{:S(2)}) collective-permute-start(bf16[64,1024]{1,0:T(8,128)(2,1)S(1)} %get-tuple-element.292.refs_0_), channel_id=1, source_target_pairs={{0,2},{1,3},{2,0},{3,1},{4,6},{5,7},{6,4},{7,5},{8,10},{9,11},{10,... | collective-permute-start | bytes 393224 | tf_op jit(solution)/shard_map/ppermute | solution.py:20
  203.9 11.0 %collective-permute-start.34 = (bf16[64,1024]{1,0:T(8,128)(2,1)S(1)}, bf16[64,1024]{1,0:T(8,128)(2,1)S(1)}, u32[]{:S(2)}, u32[]{:S(2)}) collective-permute-start(bf16[64,1024]{1,0:T(8,128)(2,1)S(1)} %get-tuple-element.292.refs_0_), channel_id=1, source_target_pairs={{0,1},{1,2},{2,3},{3,0},{4,5},{5,6},{6,7},{7,4},{8,9},{9,10},{10,1... | collective-permute-start | bytes 393224 | tf_op jit(solution)/shard_map/ppermute | solution.py:20
  204.6 10.4 %collective-permute-start.35 = (bf16[64,1024]{1,0:T(8,128)(2,1)S(1)}, bf16[64,1024]{1,0:T(8,128)(2,1)S(1)}, u32[]{:S(2)}, u32[]{:S(2)}) collective-permute-start(bf16[64,1024]{1,0:T(8,128)(2,1)S(1)} %get-tuple-element.293.refs_1_), channel_id=1, source_target_pairs={{0,12},{4,0},{8,4},{12,8},{1,13},{5,1},{9,5},{13,9},{2,14},{6,2},{... | collective-permute-start | bytes 393224 | tf_op jit(solution)/shard_map/ppermute | solution.py:20
  207.2 7.8 %collective-permute-start.36 = (bf16[64,1024]{1,0:T(8,128)(2,1)S(1)}, bf16[64,1024]{1,0:T(8,128)(2,1)S(1)}, u32[]{:S(2)}, u32[]{:S(2)}) collective-permute-start(bf16[64,1024]{1,0:T(8,128)(2,1)S(1)} %get-tuple-element.293.refs_1_), channel_id=1, source_target_pairs={{0,8},{4,12},{8,0},{12,4},{1,9},{5,13},{9,1},{13,5},{2,10},{6,14},... | collective-permute-start | bytes 393224 | tf_op jit(solution)/shard_map/ppermute | solution.py:20
  207.9 8.7 %collective-permute-start.37 = (bf16[64,1024]{1,0:T(8,128)(2,1)S(1)}, bf16[64,1024]{1,0:T(8,128)(2,1)S(1)}, u32[]{:S(2)}, u32[]{:S(2)}) collective-permute-start(bf16[64,1024]{1,0:T(8,128)(2,1)S(1)} %get-tuple-element.293.refs_1_), channel_id=1, source_target_pairs={{0,4},{4,8},{8,12},{12,0},{1,5},{5,9},{9,13},{13,1},{2,6},{6,10},{... | collective-permute-start | bytes 393224 | tf_op jit(solution)/shard_map/ppermute | solution.py:20
  216.6 60.8 %all-to-all-start.2 = ((bf16[16,472,128]{2,1,0:T(8,128)(2,1)}), bf16[16,472,128]{2,1,0:T(8,128)(2,1)}, u32[]{:S(2)}, u32[]{:S(2)}) async-start(bf16[16,472,128]{2,1,0:T(8,128)(2,1)} %copy-done.6), calls=%async_computation.3 | async-start | bytes 3866624 | tf_op jit(solution)/shard_map/all_to_all | solution.py:823
  224.4 86.0 %all-gather.7.cloned.1.call-start = ((), (), s32[]{:S(2)}) async-start(), calls=%async_computation.7 | async-start | bytes 2064384 | tf_op jit(solution)/shard_map/all_gather | solution.py:824
  226.4 48.7 %collective-permute-start.38 = (bf16[256,1024]{1,0:T(8,128)(2,1)S(1)}, bf16[256,1024]{1,0:T(8,128)(2,1)S(1)}, u32[]{:S(2)}, u32[]{:S(2)}) collective-permute-start(bf16[256,1024]{1,0:T(8,128)(2,1)S(1)} %get-tuple-element.302.refs_0_), channel_id=1, source_target_pairs={{0,12},{4,0},{8,4},{12,8},{1,13},{5,1},{9,5},{13,9},{2,14},{6,2},{... | collective-permute-start | bytes 1572872 | tf_op jit(solution)/shard_map/ppermute | solution.py:20
  229.1 46.1 %collective-permute-start.39 = (bf16[256,1024]{1,0:T(8,128)(2,1)S(1)}, bf16[256,1024]{1,0:T(8,128)(2,1)S(1)}, u32[]{:S(2)}, u32[]{:S(2)}) collective-permute-start(bf16[256,1024]{1,0:T(8,128)(2,1)S(1)} %get-tuple-element.302.refs_0_), channel_id=1, source_target_pairs={{0,4},{4,8},{8,12},{12,0},{1,5},{5,9},{9,13},{13,1},{2,6},{6,10},{... | collective-permute-start | bytes 1572872 | tf_op jit(solution)/shard_map/ppermute | solution.py:20
  229.1 48.4 %collective-permute-start.40 = (bf16[256,1024]{1,0:T(8,128)(2,1)S(1)}, bf16[256,1024]{1,0:T(8,128)(2,1)S(1)}, u32[]{:S(2)}, u32[]{:S(2)}) collective-permute-start(bf16[256,1024]{1,0:T(8,128)(2,1)S(1)} %get-tuple-element.303.refs_1_), channel_id=1, source_target_pairs={{0,3},{1,0},{2,1},{3,2},{4,7},{5,4},{6,5},{7,6},{8,11},{9,8},{10,9... | collective-permute-start | bytes 1572872 | tf_op jit(solution)/shard_map/ppermute | solution.py:20
  231.4 46.0 %collective-permute-start.41 = (bf16[256,1024]{1,0:T(8,128)(2,1)S(1)}, bf16[256,1024]{1,0:T(8,128)(2,1)S(1)}, u32[]{:S(2)}, u32[]{:S(2)}) collective-permute-start(bf16[256,1024]{1,0:T(8,128)(2,1)S(1)} %get-tuple-element.303.refs_1_), channel_id=1, source_target_pairs={{0,1},{1,2},{2,3},{3,0},{4,5},{5,6},{6,7},{7,4},{8,9},{9,10},{10,1... | collective-permute-start | bytes 1572872 | tf_op jit(solution)/shard_map/ppermute | solution.py:20
  282.4 1.9 collective-permute-start.46
  285.5 32.0 %all-to-all-start.3 = ((bf16[4,136,1024]{2,1,0:T(8,128)(2,1)}), bf16[4,136,1024]{2,1,0:T(8,128)(2,1)}, u32[]{:S(2)}, u32[]{:S(2)}) async-start(bf16[4,136,1024]{2,1,0:T(8,128)(2,1)} %broadcast_in_dim.14), calls=%async_computation.4 | async-start | bytes 2228224 | tf_op jit(solution)/shard_map/all_to_all | solution.py:842
  290.8 19.6 %collective-permute-start.42 = (bf16[128,1024]{1,0:T(8,128)(2,1)}, bf16[128,1024]{1,0:T(8,128)(2,1)S(1)}, u32[]{:S(2)}, u32[]{:S(2)}) collective-permute-start(bf16[128,1024]{1,0:T(8,128)(2,1)} %get-tuple-element.311), channel_id=1, source_target_pairs={{0,4},{4,8},{8,12},{12,0},{1,5},{5,9},{9,13},{13,1},{2,6},{6,10},{... | collective-permute-start | bytes 786440 | tf_op jit(solution)/shard_map/ppermute | solution.py:20
  291.3 19.2 %collective-permute-start.43 = (bf16[128,1024]{1,0:T(8,128)(2,1)}, bf16[128,1024]{1,0:T(8,128)(2,1)}, u32[]{:S(2)}, u32[]{:S(2)}) collective-permute-start(bf16[128,1024]{1,0:T(8,128)(2,1)} %get-tuple-element.312), channel_id=1, source_target_pairs={{0,12},{4,0},{8,4},{12,8},{1,13},{5,1},{9,5},{13,9},{2,14},{6,2},{... | collective-permute-start | bytes 786440 | tf_op jit(solution)/shard_map/ppermute | solution.py:20
  293.7 16.7 %collective-permute-start.44 = (bf16[128,1024]{1,0:T(8,128)(2,1)}, bf16[128,1024]{1,0:T(8,128)(2,1)}, u32[]{:S(2)}, u32[]{:S(2)}) collective-permute-start(bf16[128,1024]{1,0:T(8,128)(2,1)} %get-tuple-element.313), channel_id=1, source_target_pairs={{0,1},{1,2},{2,3},{3,0},{4,5},{5,6},{6,7},{7,4},{8,9},{9,10},{10,1... | collective-permute-start | bytes 786440 | tf_op jit(solution)/shard_map/ppermute | solution.py:20
  294.5 16.0 %collective-permute-start.45 = (bf16[128,1024]{1,0:T(8,128)(2,1)}, bf16[128,1024]{1,0:T(8,128)(2,1)}, u32[]{:S(2)}, u32[]{:S(2)}) collective-permute-start(bf16[128,1024]{1,0:T(8,128)(2,1)} %get-tuple-element.314), channel_id=1, source_target_pairs={{0,3},{1,0},{2,1},{3,2},{4,7},{5,4},{6,5},{7,6},{8,11},{9,8},{10,9... | collective-permute-start | bytes 786440 | tf_op jit(solution)/shard_map/ppermute | solution.py:20
  319.3 1.6 collective-permute-start.47
  (34 other events, 207.2 us)
Sparse Core Ops, SparseCore 0:
  12.6 83.2 all-gather.8
Sparse Core Ops, SparseCore 1:
  128.8 34.8 reduce-scatter.1
  179.2 97.8 all-gather.4
  278.7 31.7 all-gather.6
